TPU v7x, 256 devices: a whole 4x4x8 slice. The times are simulated.
256 devices in a mesh: sx: 32 (over y, z), sy: 8 (over x, core).
Axes of the slice: x: 4, y: 4, z: 8, core: 2. Of those that a mesh axis runs over, the one named last changes fastest.
Arguments:
- applied_loads: float32 [32, 8, 16, 192], P('sx', 'sy'), may hold values from -36 to 36
- bound_block: float32 [32, 8, 384, 384], P('sx', 'sy'), may hold values from -1 to 11, as said below
- coupling: float32 [32, 8, 384, 1152], P('sx', 'sy'), may hold values from -0.02 to 0.02
- interior_inverse: float32 [32, 8, 1152, 1152], P('sx', 'sy'), may hold values from -1 to 11, as said below
- local_inverse: float32 [32, 8, 384, 384], P('sx', 'sy'), may hold values from -1 to 11, as said below
- coarse_inverse: float32 [8192, 8192], P(('sx', 'sy')), may hold values from -1 to 11, as said below
Outputs:
- solution: float32 [32, 8, 16, 192], P('sx', 'sy')
- residual: float32 [32, 8, 16, 192], P('sx', 'sy')
- preconditioned: float32 [32, 8, 16, 192], P('sx', 'sy')
Inputs may be any that keep to these rules, and one draw needn't show every extreme that they name: bound_block is symmetric in its last two dimensions. interior_inverse is symmetric in its last two dimensions. local_inverse is symmetric in its last two dimensions. coarse_inverse is symmetric.
All inputs are finite; a program needn't handle non-finite values.
Results may differ from a plain program's by a relative error of at most 0.0003.
Values sent between devices are 32-bit elements; how exact they have to be, the bound alone decides.
A program may use at most 64 MiB of HBM per device.

v0:
```python
import jax
import jax.numpy as jnp
from jax import lax
from jax.sharding import PartitionSpec as P

F = 96
ITERS = 2


precise = lax.Precision.HIGHEST


def shifted(value, axis, by):
    count = lax.axis_size(axis)
    pairs = [(i, i + by) for i in range(count) if 0 <= i + by < count]
    return lax.ppermute(value, axis, pairs)


def matmul(left, right):
    return jnp.dot(left, right, precision=precise)


def face_copies(east_face, south_face):
    west_face = shifted(east_face, "sy", 1)
    north_face = shifted(south_face, "sx", 1)
    return jnp.concatenate([west_face, east_face, north_face, south_face], axis=1)


def owner_sums(result):
    east_back = shifted(result[:, :F], "sy", -1)
    south_back = shifted(result[:, 2 * F : 3 * F], "sx", -1)
    return (result[:, F : 2 * F] + east_back, result[:, 3 * F :] + south_back)


def exchange_faces(vector, local_map):
    result = local_map(face_copies(vector[:, :F], vector[:, F:]))
    east_total, south_total = owner_sums(result)
    return jnp.concatenate([east_total, south_total], axis=1)


def schur_local(faces, bound_matrix, coupling_matrix, interior_matrix):
    inner = matmul(faces, coupling_matrix)
    solved = matmul(inner, interior_matrix)
    back = lax.dot_general(solved, coupling_matrix, (((1,), (1,)), ((), ())), precision=precise)
    return matmul(faces, bound_matrix) - back


def coarse_part(vector, coarse_rows):
    case_count = vector.shape[0]
    coarse_count = coarse_rows.shape[0]
    run_length = vector.shape[1] // coarse_count
    group_sums = vector.reshape(case_count, coarse_count, run_length).sum(axis=2)
    correction = lax.dot_general(
        lax.all_gather(group_sums, ("sx", "sy"), axis=1, tiled=True),
        coarse_rows,
        (((1,), (1,)), ((), ())),
        precision=precise,
    )
    return jnp.repeat(correction, run_length, axis=1)


def case_dot(left, right):
    return jnp.sum(left * right, axis=1)


def shards(applied_loads, bound_block, coupling, interior_inverse, local_inverse, coarse_inverse):
    load_matrix = applied_loads[0, 0]
    bound_matrix = bound_block[0, 0]
    coupling_matrix = coupling[0, 0]
    interior_matrix = interior_inverse[0, 0]
    local_matrix = local_inverse[0, 0]

    def apply_precond(vector):
        local_part = exchange_faces(vector, lambda faces: matmul(faces, local_matrix))
        return local_part + coarse_part(vector, coarse_inverse)

    def local_dot(left, right):
        return case_dot(left, right)

    def residual_dots(left, right):
        return lax.psum(local_dot(left, right), ("sx", "sy"))

    solution = jnp.zeros_like(load_matrix)
    residual = load_matrix
    preconditioned = apply_precond(residual)
    precond_dot = residual_dots(residual, preconditioned)
    direction = preconditioned
    for step_index in range(ITERS):
        image_dir = exchange_faces(
            direction,
            lambda faces: schur_local(faces, bound_matrix, coupling_matrix, interior_matrix),
        )
        step_size = precond_dot / lax.psum(local_dot(direction, image_dir), ("sx", "sy"))
        solution = solution + step_size[:, None] * direction
        residual = residual - step_size[:, None] * image_dir
        preconditioned = apply_precond(residual)
        if step_index + 1 < ITERS:
            next_dot = residual_dots(residual, preconditioned)
            direction = preconditioned + (next_dot / precond_dot)[:, None] * direction
            precond_dot = next_dot
    return (solution[None, None], residual[None, None], preconditioned[None, None])


def solution(mesh):
    placed = (
        P("sx", "sy", None, None),
        P("sx", "sy", None, None),
        P("sx", "sy", None, None),
        P("sx", "sy", None, None),
        P("sx", "sy", None, None),
        P(("sx", "sy"), None),
    )
    return jax.shard_map(
        shards,
        mesh=mesh,
        in_specs=placed,
        out_specs=(P("sx", "sy", None, None), P("sx", "sy", None, None), P("sx", "sy", None, None)),
        check_vma=False,
    )
```

profile of v0, /device:TPU:1, one launch (start us, length us, event | category | flops | bytes accessed | tf_op | source)
XLA Modules:
  0.0 610.9 jit_solution(16749747966216720537)
XLA Ops:
  1.6 4.4 collective-permute-start.1
  6.0 4.0 collective-permute-start
  10.9 1.5 fusion.18
  12.4 1.9 collective-permute-start.2
  14.3 72.5 %all-gather = f32[256,32,16]{1,2,0:T(8,128)S(1)} all-gather(f32[1,32,16]{1,2,0:T(8,128)S(1)} %copy.91), channel_id=1, replica_groups=mesh['sx'=32,'sy'=8] {'sx','sy'}, dimensions={0}, use_global_device_ids=true | all-gather | bytes 526336 | tf_op jit(solution)/shard_map/all_gather | solution.py:54
  86.9 2.0 copy.92
  88.9 2.6 reshape.343
  94.0 2.0 collective-permute-done.3
  96.8 2.7 collective-permute-start.5
  99.5 3.5 collective-permute-start.4
  104.6 5.1 fusion.2
  109.8 1.6 fusion.8
  113.2 3.5 collective-permute-done.7
  117.4 2.3 collective-permute-start.6
  136.2 79.5 %all-reduce = (f32[16]{0:T(128)}, f32[16]{0:T(128)}) all-reduce(f32[16]{0:T(128)} %get-tuple-element.5, f32[16]{0:T(128)} %multiply_reduce_fusion), channel_id=1, replica_groups=mesh['sx'=32,'sy'=8] {'sx','sy'}, use_global_device_ids=true, to_apply=%region_2.0 | all-reduce | flops 32 | bytes 256 | tf_op jit(solution)/shard_map/psum | solution.py:81
  218.4 2.8 collective-permute-start.9
  221.2 3.3 collective-permute-start.8
  224.5 1.6 fusion.23
  229.2 1.9 collective-permute-start.10
  231.1 68.1 %all-gather.1 = f32[256,32,16]{1,2,0:T(8,128)S(1)} all-gather(f32[1,32,16]{1,2,0:T(8,128)} %copy.100), channel_id=1, replica_groups=mesh['sx'=32,'sy'=8] {'sx','sy'}, dimensions={0}, use_global_device_ids=true | all-gather | bytes 526336 | tf_op jit(solution)/shard_map/all_gather | solution.py:54
  299.3 2.0 copy.101
  301.3 3.4 reshape.345
  307.4 2.0 fusion.67
  310.7 1.6 reshape.339
  312.2 1.6 copy.103
  315.1 1.5 multiply_reduce_fusion.1
  316.6 75.3 %psum.30 = f32[16]{0:T(128)} all-reduce(f32[16]{0:T(128)} %multiply_reduce_fusion.1), channel_id=1, replica_groups=mesh['sx'=32,'sy'=8] {'sx','sy'}, use_global_device_ids=true, to_apply=%region_7.0 | all-reduce | flops 16 | bytes 128 | tf_op jit(solution)/shard_map/psum | solution.py:81
  393.6 3.5 collective-permute-start.13
  397.1 3.5 collective-permute-start.12
  402.1 5.1 fusion
  407.3 1.6 fusion.4
  410.7 3.1 collective-permute-done.15
  414.5 2.3 collective-permute-start.14
  416.8 1.6 reshape.338
  418.3 1.6 copy.99
  419.9 1.6 reshape.340
  436.5 1.6 fusion.22
  438.1 1.6 copy.108
  439.7 77.8 %psum.31 = f32[16]{0:T(128)} all-reduce(f32[16]{0:T(128)} %fusion.22), channel_id=1, replica_groups=mesh['sx'=32,'sy'=8] {'sx','sy'}, use_global_device_ids=true, to_apply=%region_9.0 | all-reduce | flops 16 | bytes 128 | tf_op jit(solution)/shard_map/psum | solution.py:93
  518.2 1.6 subtract_reduce_fusion
  521.5 1.7 collective-permute-start.17
  523.2 3.9 collective-permute-start.16
  527.1 66.9 %all-gather.2 = f32[256,32,16]{1,2,0:T(8,128)S(1)} all-gather(f32[1,32,16]{1,2,0:T(8,128)S(1)} %copy.109), channel_id=1, replica_groups=mesh['sx'=32,'sy'=8] {'sx','sy'}, dimensions={0}, use_global_device_ids=true | all-gather | bytes 526336 | tf_op jit(solution)/shard_map/all_gather | solution.py:54
  594.0 2.0 copy.110
  596.1 3.4 reshape.347
  600.7 2.1 collective-permute-start.18
  602.8 2.0 fusion.68
  608.0 2.2 collective-permute-done.19
  (161 shorter events, 64.9 us)
Async XLA Ops:
  0.6 103.0 %copy-start = (f32[1,1,384,1152]{3,2,1,0:T(8,128)S(1)}, f32[1,1,384,1152]{3,2,1,0:T(8,128)}, u32[]{:S(2)}) copy-start(f32[1,1,384,1152]{3,2,1,0:T(8,128)} %param.8) | copy-start | bytes 5308420
  1.6 9.3 %collective-permute-start.1 = (f32[16,96]{1,0:T(8,128)S(1)}, f32[16,96]{1,0:T(8,128)S(1)}, u32[]{:S(2)}, u32[]{:S(2)}) collective-permute-start(f32[16,96]{1,0:T(8,128)S(1)} %get-tuple-element.26), channel_id=1, source_target_pairs={{0,8},{8,16},{16,24},{24,32},{32,40},{40,48},{48,56},{56,64},{64,7... | collective-permute-start | bytes 18440 | tf_op jit(solution)/shard_map/ppermute | solution.py:16
  6.0 4.9 collective-permute-start
  12.4 79.1 %collective-permute-start.2 = (f32[16,96]{1,0:T(8,128)S(1)}, f32[16,96]{1,0:T(8,128)S(1)}, u32[]{:S(2)}, u32[]{:S(2)}) collective-permute-start(f32[16,96]{1,0:T(8,128)S(1)} %slice.123), channel_id=1, source_target_pairs={{1,0},{2,1},{3,2},{4,3},{5,4},{6,5},{7,6},{9,8},{10,9},{11,10},{12... | collective-permute-start | bytes 18440 | tf_op jit(solution)/shard_map/ppermute | solution.py:16
  88.9 4.0 copy-start.1
  88.9 7.2 %copy-start.8 = (f32[1,1,16,192]{3,2,1,0:T(8,128)S(1)}, f32[1,1,16,192]{3,2,1,0:T(8,128)}, u32[]{:S(2)}) copy-start(f32[1,1,16,192]{3,2,1,0:T(8,128)} %param.6) | copy-start | bytes 36868
  91.6 13.0 %copy-start.23 = (f32[16,96]{1,0:T(8,128)}, f32[16,96]{1,0:T(8,128)S(1)}, u32[]{:S(2)}) copy-start(f32[16,96]{1,0:T(8,128)S(1)} %get-tuple-element.15) | copy-start | bytes 18436
  91.6 4.4 collective-permute-start.3
  93.8 10.7 %copy-start.9 = (f32[16,32]{0,1:T(8,128)}, f32[16,32]{0,1:T(8,128)S(1)}, u32[]{:S(2)}) copy-start(f32[16,32]{0,1:T(8,128)S(1)} %fusion.66) | copy-start | bytes 6148
  93.9 10.7 %copy-start.6 = (f32[16,32,6]{0,2,1:T(8,128)}, f32[16,32,6]{0,2,1:T(8,128)S(1)}, u32[]{:S(2)}) copy-start(f32[16,32,6]{0,2,1:T(8,128)S(1)} %broadcast_in_dim.6) | copy-start | bytes 36868
  96.0 8.6 %copy-start.25 = (f32[16,96]{1,0:T(8,128)}, f32[16,96]{1,0:T(8,128)S(1)}, u32[]{:S(2)}) copy-start(f32[16,96]{1,0:T(8,128)S(1)} %slice_add_fusion.8) | copy-start | bytes 18436
  96.8 7.9 %copy-start.15 = (f32[16,192]{1,0:T(8,128)}, f32[16,192]{1,0:T(8,128)S(1)}, u32[]{:S(2)}) copy-start(f32[16,192]{1,0:T(8,128)S(1)} %get-tuple-element.6) | copy-start | bytes 36868
  96.8 6.2 %collective-permute-start.5 = (f32[16,96]{1,0:T(8,128)S(1)}, f32[16,96]{1,0:T(8,128)S(1)}, u32[]{:S(2)}, u32[]{:S(2)}) collective-permute-start(f32[16,96]{1,0:T(8,128)S(1)} %get-tuple-element.24), channel_id=1, source_target_pairs={{0,8},{8,16},{16,24},{24,32},{32,40},{40,48},{48,56},{56,64},{64,7... | collective-permute-start | bytes 18440 | tf_op jit(solution)/shard_map/ppermute | solution.py:16
  99.5 4.1 collective-permute-start.4
  109.7 1.6 copy-start.3
  109.8 117.7 %copy-start.2 = (f32[1,1,384,384]{3,2,1,0:T(8,128)S(1)}, f32[1,1,384,384]{3,2,1,0:T(8,128)}, u32[]{:S(2)}) copy-start(f32[1,1,384,384]{3,2,1,0:T(8,128)} %param.10) | copy-start | bytes 1769476
  111.8 4.8 copy-start.18
  111.9 4.8 collective-permute-start.7
  117.4 10.8 %collective-permute-start.6 = (f32[16,96]{1,0:T(8,128)}, f32[16,96]{1,0:T(8,128)}, u32[]{:S(2)}, u32[]{:S(2)}) collective-permute-start(f32[16,96]{1,0:T(8,128)} %get-tuple-element.14), channel_id=1, source_target_pairs={{1,0},{2,1},{3,2},{4,3},{5,4},{6,5},{7,6},{9,8},{10,9},{11,10},{12... | collective-permute-start | bytes 18440 | tf_op jit(solution)/shard_map/ppermute | solution.py:16
  216.3 8.1 %copy-start.29 = (f32[16]{0:T(128)}, f32[16]{0:T(128)S(1)}, u32[]{:S(2)}) copy-start(f32[16]{0:T(128)S(1)} %div.9) | copy-start | bytes 196
  218.4 9.0 %collective-permute-start.9 = (f32[16,96]{1,0:T(8,128)}, f32[16,96]{1,0:T(8,128)}, u32[]{:S(2)}, u32[]{:S(2)}) collective-permute-start(f32[16,96]{1,0:T(8,128)} %get-tuple-element.22), channel_id=1, source_target_pairs={{0,8},{8,16},{16,24},{24,32},{32,40},{40,48},{48,56},{56,64},{64,7... | collective-permute-start | bytes 18440 | tf_op jit(solution)/shard_map/ppermute | solution.py:16
  221.2 6.2 %collective-permute-start.8 = (f32[16,96]{1,0:T(8,128)}, f32[16,96]{1,0:T(8,128)}, u32[]{:S(2)}, u32[]{:S(2)}) collective-permute-start(f32[16,96]{1,0:T(8,128)} %get-tuple-element.21), channel_id=1, source_target_pairs={{0,1},{1,2},{2,3},{3,4},{4,5},{5,6},{6,7},{8,9},{9,10},{10,11},{11... | collective-permute-start | bytes 18440 | tf_op jit(solution)/shard_map/ppermute | solution.py:16
  229.2 75.4 %collective-permute-start.10 = (f32[16,96]{1,0:T(8,128)}, f32[16,96]{1,0:T(8,128)}, u32[]{:S(2)}, u32[]{:S(2)}) collective-permute-start(f32[16,96]{1,0:T(8,128)} %slice.135), channel_id=1, source_target_pairs={{1,0},{2,1},{3,2},{4,3},{5,4},{6,5},{7,6},{9,8},{10,9},{11,10},{12... | collective-permute-start | bytes 18440 | tf_op jit(solution)/shard_map/ppermute | solution.py:16
  306.1 7.7 %collective-permute-start.11 = (f32[16,96]{1,0:T(8,128)}, f32[16,96]{1,0:T(8,128)}, u32[]{:S(2)}, u32[]{:S(2)}) collective-permute-start(f32[16,96]{1,0:T(8,128)} %get-tuple-element.12), channel_id=1, source_target_pairs={{8,0},{16,8},{24,16},{32,24},{40,32},{48,40},{56,48},{64,56},{72,6... | collective-permute-start | bytes 18440 | tf_op jit(solution)/shard_map/ppermute | solution.py:16
  392.7 8.0 %copy-start.31 = (f32[16]{0:T(128)}, f32[16]{0:T(128)S(1)}, u32[]{:S(2)}) copy-start(f32[16]{0:T(128)S(1)} %div.10) | copy-start | bytes 196
  393.6 7.1 %collective-permute-start.13 = (f32[16,96]{1,0:T(8,128)S(1)}, f32[16,96]{1,0:T(8,128)S(1)}, u32[]{:S(2)}, u32[]{:S(2)}) collective-permute-start(f32[16,96]{1,0:T(8,128)S(1)} %get-tuple-element.20), channel_id=1, source_target_pairs={{0,8},{8,16},{16,24},{24,32},{32,40},{40,48},{48,56},{56,64},{64,7... | collective-permute-start | bytes 18440 | tf_op jit(solution)/shard_map/ppermute | solution.py:16
  397.1 4.0 collective-permute-start.12
  409.3 4.5 copy-start.17
  409.4 4.4 collective-permute-start.15
  414.5 15.5 %collective-permute-start.14 = (f32[16,96]{1,0:T(8,128)}, f32[16,96]{1,0:T(8,128)}, u32[]{:S(2)}, u32[]{:S(2)}) collective-permute-start(f32[16,96]{1,0:T(8,128)} %get-tuple-element.10), channel_id=1, source_target_pairs={{1,0},{2,1},{3,2},{4,3},{5,4},{6,5},{7,6},{9,8},{10,9},{11,10},{12... | collective-permute-start | bytes 18440 | tf_op jit(solution)/shard_map/ppermute | solution.py:16
  518.2 2.5 copy-start.33
  521.5 78.1 %collective-permute-start.17 = (f32[16,96]{1,0:T(8,128)S(1)}, f32[16,96]{1,0:T(8,128)S(1)}, u32[]{:S(2)}, u32[]{:S(2)}) collective-permute-start(f32[16,96]{1,0:T(8,128)S(1)} %get-tuple-element.18), channel_id=1, source_target_pairs={{0,8},{8,16},{16,24},{24,32},{32,40},{40,48},{48,56},{56,64},{64,7... | collective-permute-start | bytes 18440 | tf_op jit(solution)/shard_map/ppermute | solution.py:16
  523.2 76.3 %collective-permute-start.16 = (f32[16,96]{1,0:T(8,128)S(1)}, f32[16,96]{1,0:T(8,128)}, u32[]{:S(2)}, u32[]{:S(2)}) collective-permute-start(f32[16,96]{1,0:T(8,128)S(1)} %get-tuple-element.17), channel_id=1, source_target_pairs={{0,1},{1,2},{2,3},{3,4},{4,5},{5,6},{6,7},{8,9},{9,10},{10,11},{11... | collective-permute-start | bytes 18440 | tf_op jit(solution)/shard_map/ppermute | solution.py:16
  596.0 11.0 %copy-start.11 = (f32[16,96]{1,0:T(8,128)S(1)}, f32[16,96]{1,0:T(8,128)}, u32[]{:S(2)}) copy-start(f32[16,96]{1,0:T(8,128)} %get-tuple-element.11) | copy-start | bytes 18436
  596.1 11.0 %copy-start.13 = (f32[16,96]{1,0:T(8,128)S(1)}, f32[16,96]{1,0:T(8,128)}, u32[]{:S(2)}) copy-start(f32[16,96]{1,0:T(8,128)} %copy-done.12) | copy-start | bytes 18436
  596.1 11.0 %copy-start.19 = (f32[16,96]{1,0:T(8,128)S(1)}, f32[16,96]{1,0:T(8,128)}, u32[]{:S(2)}) copy-start(f32[16,96]{1,0:T(8,128)} %get-tuple-element.13) | copy-start | bytes 18436
  596.1 11.0 %copy-start.20 = (f32[16,96]{1,0:T(8,128)S(1)}, f32[16,96]{1,0:T(8,128)}, u32[]{:S(2)}) copy-start(f32[16,96]{1,0:T(8,128)} %slice_add_fusion.7) | copy-start | bytes 18436
  596.1 11.0 %copy-start.21 = (f32[16,96]{1,0:T(8,128)S(1)}, f32[16,96]{1,0:T(8,128)}, u32[]{:S(2)}) copy-start(f32[16,96]{1,0:T(8,128)} %get-tuple-element.9) | copy-start | bytes 18436
  596.1 11.0 %copy-start.22 = (f32[16,96]{1,0:T(8,128)S(1)}, f32[16,96]{1,0:T(8,128)}, u32[]{:S(2)}) copy-start(f32[16,96]{1,0:T(8,128)} %slice_add_fusion.3) | copy-start | bytes 18436
  596.1 11.0 %copy-start.24 = (f32[16,96]{1,0:T(8,128)S(1)}, f32[16,96]{1,0:T(8,128)}, u32[]{:S(2)}) copy-start(f32[16,96]{1,0:T(8,128)} %copy-done.23) | copy-start | bytes 18436
  596.1 11.0 %copy-start.26 = (f32[16,96]{1,0:T(8,128)S(1)}, f32[16,96]{1,0:T(8,128)}, u32[]{:S(2)}) copy-start(f32[16,96]{1,0:T(8,128)} %copy-done.25) | copy-start | bytes 18436
  596.1 11.0 %copy-start.27 = (f32[1,1,16,192]{3,2,1,0:T(8,128)S(1)}, f32[1,1,16,192]{3,2,1,0:T(8,128)}, u32[]{:S(2)}) copy-start(f32[1,1,16,192]{3,2,1,0:T(8,128)} %copy.99) | copy-start | bytes 36868
  599.5 7.6 %copy-start.28 = (f32[1,1,16,192]{3,2,1,0:T(8,128)S(1)}, f32[1,1,16,192]{3,2,1,0:T(8,128)}, u32[]{:S(2)}) copy-start(f32[1,1,16,192]{3,2,1,0:T(8,128)} %copy.108) | copy-start | bytes 36868
  599.5 7.6 %copy-start.30 = (f32[16]{0:T(128)S(1)}, f32[16]{0:T(128)}, u32[]{:S(2)}) copy-start(f32[16]{0:T(128)} %copy-done.29) | copy-start | bytes 196
  599.5 7.6 %copy-start.32 = (f32[16]{0:T(128)S(1)}, f32[16]{0:T(128)}, u32[]{:S(2)}) copy-start(f32[16]{0:T(128)} %copy-done.31) | copy-start | bytes 196
  599.5 7.6 %copy-start.34 = (f32[16]{0:T(128)S(1)}, f32[16]{0:T(128)}, u32[]{:S(2)}) copy-start(f32[16]{0:T(128)} %copy-done.33) | copy-start | bytes 196
  600.7 5.0 collective-permute-start.18
  605.8 4.4 collective-permute-start.19
  (7 other events, 5.4 us)
where the time goes:
time: 614 us; the launch traced here: 611 us
  blocking collectives  440 us (72%)
  local copies, waits for them, and re-layouts  60.5 us (10%)
  starting transfers between devices  50.1 us (8%)
  matrix products  25 us (4%)
  other arithmetic  21 us (3%)
  waiting for transfers between devices  12.7 us (2%)
    all_gather x3, blocking collectives, coarse_part(): lax.all_gather(group_sums, ('sx', 'sy'), axis=1, tiled=True)  208 us
    psum x2, blocking collectives, residual_dots(): return lax.psum(local_dot(left, right), ('sx', 'sy'))  155 us
    psum x1, blocking collectives, shards(): lax.psum(local_dot(direction, image_dir), ('sx', 'sy'))  77.8 us
    ppermute x20, starting transfers between devices, shifted(): return lax.ppermute(value, axis, pairs)  50.1 us
    unnamed x79, local copies, waits for them, and re-layouts  17.4 us
    dot_general x9, matrix products, matmul(): return jnp.dot(left, right, precision=precise)  16.9 us
    concatenate x10, local copies, waits for them, and re-layouts, exchange_faces(): return jnp.concatenate([east_total, south_total], axis=1)  13.1 us
    ppermute x20, waiting for transfers between devices, shifted(): return lax.ppermute(value, axis, pairs)  12.7 us
  transfers between devices with their start and end apart: 20, of which 7 were waited for; matrix products, arithmetic and copies ran while one was open for 8% of the time, Pallas kernels for 0%

commit v1 on v0

v1 whole, which is shorter than its diff:
```python
import jax
import jax.numpy as jnp
from jax import lax
from jax.experimental import pallas as pl
from jax.experimental.pallas import tpu as pltpu
from jax.sharding import PartitionSpec as P

MESH = pl.DeviceIdType.MESH
F = 96
FP = 128
FACES = 4
K = 16
NF = FACES * F
NP = FACES * FP
NI = 1152
NC = 8192
LX, LY, LZ = 4, 4, 8
COLS = 384
f32, bf16 = jnp.float32, jnp.bfloat16

LOADS_W, LOADS_N = 0, 1
PRE0, PRE1, PRE2 = 2, 4, 6
Z0, Z1 = 8, 10
SCH0, SCH1 = 12, 16
SLOTS = 20


def split(value):
    high = value.astype(bf16)
    low = (value - high.astype(f32)).astype(bf16)
    return high, low


def dot(left, right):
    return jnp.dot(left, right, preferred_element_type=f32)


def dot_t(left, right):
    return lax.dot_general(left, right, (((1,), (1,)), ((), ())), preferred_element_type=f32)


def pad_split(get_block, high_ref, low_ref):
    high_ref[...] = jnp.zeros_like(high_ref)
    low_ref[...] = jnp.zeros_like(low_ref)
    for a in range(FACES):
        for b in range(FACES):
            high, low = split(get_block(a, b))
            high_ref[a * FP : a * FP + F, b * FP : b * FP + F] = high
            low_ref[a * FP : a * FP + F, b * FP : b * FP + F] = low


def apply_local(faces, high_ref, low_ref):
    high, low = split(jnp.concatenate(faces, axis=1))
    both = dot(jnp.concatenate([high, low], axis=0), high_ref[...])
    result = both[:K] + both[K:] + dot(high, low_ref[...])
    return [result[:, f * FP : (f + 1) * FP] for f in range(FACES)]


def kernel(
    loads_ref, bound_ref, coupling_ref, interior_ref, local_ref, coarse_ref,
    x_ref, r_ref, z_ref,
    loads_v, bound_v, coupling_v, interior_v, local_v, coarse_v, load_sem,
    l_high, l_low, s_high, s_low, c_high, c_low, i_high, i_low, t_high, t_low, schur_v,
    permuted, partner_rows, coarse_w,
    line_v, plane_v, part_out, part_in, halo_out, halo_in,
    line_send, line_recv, plane_send, plane_recv, swap_send, swap_recv, part_send, part_recv, halo_send, halo_recv,
):
    i = lax.axis_index("sx")
    j = lax.axis_index("sy")
    y, z = lax.div(i, LZ), lax.rem(i, LZ)
    x, core = lax.div(j, 2), lax.rem(j, 2)
    block = y * LX + x
    east = {"sx": i, "sy": lax.rem(j + 1, 2 * LX)}
    west = {"sx": i, "sy": lax.rem(j + 2 * LX - 1, 2 * LX)}
    south = {"sx": lax.rem(i + 1, LY * LZ), "sy": j}
    north = {"sx": lax.rem(i + LY * LZ - 1, LY * LZ), "sy": j}
    partner = {"sx": i, "sy": x * 2 + (1 - core)}
    line = [{"sx": y * LZ + lax.rem(z + s, LZ), "sy": j} for s in range(1, LZ)]
    plane = [
        {"sx": lax.rem(y + s // LX, LY) * LZ + z, "sy": lax.rem(x + s % LX, LX) * 2 + core} for s in range(1, LX * LY)
    ]

    barrier = pltpu.get_barrier_semaphore()
    greeted = [east, west, south, north, partner] + line + plane
    for device in greeted:
        pl.semaphore_signal(barrier, 1, device_id=device, device_id_type=MESH)

    fetches = [
        pltpu.make_async_copy(source, target, load_sem.at[k])
        for k, (source, target) in enumerate(
            [
                (loads_ref.at[0, 0], loads_v),
                (coarse_ref, coarse_v),
                (local_ref.at[0, 0], local_v),
                (coupling_ref.at[0, 0], coupling_v),
                (interior_ref.at[0, 0], interior_v),
                (bound_ref.at[0, 0], bound_v),
            ]
        )
    ]
    for fetch in fetches:
        fetch.start()

    has_west, has_east = j > 0, j < 2 * LX - 1
    has_north, has_south = i > 0, i < LY * LZ - 1

    def halo_copy(slot, device):
        return pltpu.make_async_remote_copy(
            halo_out.at[slot], halo_in.at[slot], halo_send.at[slot], halo_recv.at[slot], device_id=device, device_id_type=MESH
        )

    def halo_start(slot, device, value):
        halo_out[slot] = value
        copy = halo_copy(slot, device)
        copy.start()
        started.append(copy)

    def halo_wait(slot, device, present):
        halo_copy(slot, device).wait_recv()
        return jnp.where(present, halo_in[slot], 0.0)

    started = []

    lane_row = lax.broadcasted_iota(jnp.int32, (1, FP), 1)
    lane_group = lane_row // 32
    value_lane = lax.broadcasted_iota(jnp.int32, (2 * FP, FP), 0)
    coarse_lane = lax.broadcasted_iota(jnp.int32, (2 * FP, FP), 1) % 32
    in_face = value_lane % FP
    run_of = (value_lane // FP) * 16 + in_face // 6
    restrict = ((run_of == coarse_lane) & (in_face < F)).astype(f32).astype(bf16)
    coarse_at = lax.broadcasted_iota(jnp.int32, (FP, 2 * FP), 0)
    value_at = lax.broadcasted_iota(jnp.int32, (FP, 2 * FP), 1)
    value_in = value_at % FP
    spread_of = (value_at // FP) * 16 + value_in // 6
    spread = ((spread_of == coarse_at % 64) & (value_in < F)).astype(f32).astype(bf16)

    def line_copy(phase, s):
        return pltpu.make_async_remote_copy(
            line_v.at[phase, z], line_v.at[phase, z], line_send.at[phase, s], line_recv.at[phase, s],
            device_id=line[s - 1], device_id_type=MESH,
        )

    def plane_copy(phase, s):
        return pltpu.make_async_remote_copy(
            plane_v.at[phase, block], plane_v.at[phase, block], plane_send.at[phase, s], plane_recv.at[phase, s],
            device_id=plane[s - 1], device_id_type=MESH,
        )

    def part_copy(phase):
        return pltpu.make_async_remote_copy(
            part_out.at[phase], part_in.at[phase], part_send.at[phase], part_recv.at[phase],
            device_id=partner, device_id_type=MESH,
        )

    def gather_prepare(phase, east_face, south_face, dots):
        value = jnp.concatenate([east_face, south_face], axis=1)
        high, rest = value.astype(bf16), None
        rest = value - high.astype(f32)
        middle, low = split(rest)
        sums = dot(jnp.concatenate([high, middle, low], axis=0), restrict)
        sums = sums[:K] + sums[K : 2 * K] + sums[2 * K :]
        packed = jnp.zeros((4, FP), f32)
        for q in range(4):
            packed = jnp.where(lane_group == q, sums[4 * q : 4 * q + 4], packed)
        placed = jnp.zeros((K, FP), f32)
        case = lax.broadcasted_iota(jnp.int32, (K, FP), 0)
        lane = lax.broadcasted_iota(jnp.int32, (K, FP), 1)
        for d, (left, right) in enumerate(dots):
            product = left[0] * right[0] + left[1] * right[1]
            placed = jnp.where(lane == d * K + case, jnp.sum(product, axis=1, keepdims=True), placed)
        row = jnp.sum(placed, axis=0, keepdims=True)
        line_v[phase, z] = jnp.concatenate([packed, jnp.broadcast_to(row, (4, FP))], axis=0)

    def gather_start(phase):
        for s in range(1, LZ):
            copy = line_copy(phase, s)
            copy.start()
            started.append(copy)

    def gather_forward(phase):
        for s in range(1, LZ):
            line_copy(phase, s).wait_recv()
        tiles = [line_v[phase, s] for s in range(LZ)]
        for h in range(2):
            rows = []
            for q in range(4):
                mixed = jnp.zeros((8, FP), f32)
                for d in range(4):
                    turn = ((d - q) % 4) * 32
                    tile = tiles[4 * h + d]
                    turned = pltpu.roll(tile, turn, 1) if turn else tile
                    mixed = jnp.where(lane_group == d, turned, mixed)
                rows.append(mixed[:4])
            plane_v[phase, block, h * K : (h + 1) * K] = jnp.concatenate(rows, axis=0)
        total = tiles[0]
        for s in range(1, LZ):
            total = total + tiles[s]
        plane_v[phase, block, 2 * K :] = total
        for s in range(1, LX * LY):
            copy = plane_copy(phase, s)
            copy.start()
            started.append(copy)

    def gather_finish(phase):
        for s in range(1, LX * LY):
            plane_copy(phase, s).wait_recv()
        total = jnp.zeros((2 * K, FP), f32)
        sums = jnp.zeros((8, FP), f32)
        for b in range(LX * LY):
            value = jnp.concatenate([plane_v[phase, b, :K], plane_v[phase, b, K : 2 * K]], axis=1)
            high, low = split(value)
            total += dot_t(jnp.concatenate([high, low], axis=0), coarse_w[:, b * 256 : (b + 1) * 256])
            sums += plane_v[phase, b, 2 * K :]
        part = total[:K] + total[K:]
        part_out[phase, :K] = part
        part_out[phase, K:] = sums
        copy = part_copy(phase)
        copy.start()
        started.append(copy)
        part_copy(phase).wait_recv()
        own = part + pltpu.roll(part_in[phase, :K], FP - 32, 1)
        sums = sums + part_in[phase, K:]
        high, low = split(own)
        wide = dot(jnp.concatenate([high, low], axis=0), spread)
        wide = wide[:K] + wide[K:]
        case = lax.broadcasted_iota(jnp.int32, (K, FP), 0)
        lane = lax.broadcasted_iota(jnp.int32, (K, FP), 1)

        def column(d):
            return jnp.sum(jnp.where(lane == d * K + case, sums[4:5], 0.0), axis=1, keepdims=True)

        return wide[:, :FP], wide[:, FP:], column

    def precond_local(phase, slot, faces):
        result = apply_local(faces, l_high, l_low)
        halo_start(slot, west, result[0])
        halo_start(slot + 1, north, result[2])
        return result[1], result[3]

    def precond_finish(phase, slot, mine):
        add_east = halo_wait(slot, west, has_east)
        add_south = halo_wait(slot + 1, north, has_south)
        wide_east, wide_south, column = gather_finish(phase)
        return mine[0] + add_east + wide_east, mine[1] + add_south + wide_south, column

    def share_faces(slot, value):
        halo_start(slot, east, value[0])
        halo_start(slot + 1, south, value[1])
        from_west = halo_wait(slot, east, has_west)
        from_north = halo_wait(slot + 1, south, has_north)
        return [from_west, value[0], from_north, value[1]]

    def schur(slot, faces):
        result = apply_local(faces, s_high, s_low)
        halo_start(slot, west, result[0])
        halo_start(slot + 1, north, result[2])
        halo_start(slot + 2, east, result[1])
        halo_start(slot + 3, south, result[3])
        east_total = result[1] + halo_wait(slot, west, has_east)
        south_total = result[3] + halo_wait(slot + 1, north, has_south)
        west_total = jnp.where(has_west, result[0] + halo_wait(slot + 2, east, has_west), 0.0)
        north_total = jnp.where(has_north, result[2] + halo_wait(slot + 3, south, has_north), 0.0)
        return [west_total, east_total, north_total, south_total]

    fetches[0].wait()
    padding = jnp.zeros((K, FP - F), f32)
    r0 = (
        jnp.concatenate([loads_v[:, :F], padding], axis=1),
        jnp.concatenate([loads_v[:, F : 2 * F], padding], axis=1),
    )
    gather_prepare(0, r0[0], r0[1], [])
    pl.semaphore_wait(barrier, len(greeted))
    gather_start(0)
    halo_start(LOADS_W, east, r0[0])
    halo_start(LOADS_N, south, r0[1])

    fetches[1].wait()

    def permute(step, _):
        y_at, rest = lax.div(step, 4), lax.rem(step, 4)
        half, j_half = lax.div(rest, 2), lax.rem(rest, 2)
        tiles = []
        for d in range(4):
            at = ((y_at * LZ + half * 4 + d) * 2 + j_half) * FP
            tiles.append(coarse_v[:, pl.ds(pl.multiple_of(at, FP), FP)])
        for q in range(4):
            mixed = tiles[q] if q == 0 else pltpu.roll(tiles[0], ((0 - q) % 4) * 32, 1)
            for d in range(1, 4):
                turn = ((d - q) % 4) * 32
                turned = pltpu.roll(tiles[d], turn, 1) if turn else tiles[d]
                mixed = jnp.where(lane_group == d, turned, mixed)
            at = (y_at * LX + j_half * 2 + q // 2) * 256 + half * FP
            permuted[q % 2, :, pl.ds(pl.multiple_of(at, FP), FP)] = mixed
        return 0

    lax.fori_loop(0, 16, permute, 0)
    swap = pltpu.make_async_remote_copy(
        permuted.at[1 - core], partner_rows, swap_send, swap_recv, device_id=partner, device_id_type=MESH
    )
    swap.start()
    started.append(swap)

    fetches[2].wait()
    pad_split(lambda a, b: local_v[a * F : (a + 1) * F, b * F : (b + 1) * F], l_high, l_low)
    from_west = halo_wait(LOADS_W, east, has_west)
    from_north = halo_wait(LOADS_N, south, has_north)
    mine = precond_local(0, PRE0, [from_west, r0[0], from_north, r0[1]])

    gather_forward(0)

    high, low = split(permuted[core])
    coarse_w[0:32], coarse_w[64:96] = high, low
    swap.wait_recv()
    high, low = split(partner_rows[...])
    coarse_w[32:64], coarse_w[96:128] = high, low

    fetches[3].wait()
    c_high[...], c_low[...] = split(coupling_v[...])
    fetches[4].wait()

    def times_interior(step, _):
        columns = pl.ds(pl.multiple_of(step * COLS, FP), COLS)
        i_high[...], i_low[...] = split(interior_v[:, columns])
        total = dot(c_high[...], i_high[...]) + dot(c_low[...], i_high[...]) + dot(c_high[...], i_low[...])
        t_high[:, columns], t_low[:, columns] = split(total)
        return 0

    lax.fori_loop(0, NI // COLS, times_interior, 0)
    back = dot_t(t_high[...], c_high[...]) + dot_t(t_low[...], c_high[...]) + dot_t(t_high[...], c_low[...])
    fetches[5].wait()
    schur_v[...] = bound_v[...] - back
    pad_split(lambda a, b: schur_v[a * F : (a + 1) * F, b * F : (b + 1) * F], s_high, s_low)

    z0_east, z0_south, _ = precond_finish(0, PRE0, mine)
    z0 = (z0_east, z0_south)

    q0_faces = schur(SCH0, share_faces(Z0, z0))
    q0 = (q0_faces[1], q0_faces[3])
    gather_prepare(1, q0[0], q0[1], [(r0, z0), (z0, q0)])
    gather_start(1)
    mine = precond_local(1, PRE1, q0_faces)
    gather_forward(1)
    w0_east, w0_south, column = precond_finish(1, PRE1, mine)
    w0 = (w0_east, w0_south)
    rz0, dq0 = column(0), column(1)
    step0 = rz0 / dq0
    z1 = tuple(a - step0 * b for a, b in zip(z0, w0))

    z1_faces = share_faces(Z1, z1)
    r1 = tuple(a - step0 * b for a, b in zip(r0, q0))
    t1_faces = schur(SCH1, z1_faces)
    t1 = (t1_faces[1], t1_faces[3])
    gather_prepare(2, t1[0], t1[1], [(r1, z1), (z1, t1), (z0, t1), (z1, q0)])
    gather_start(2)
    mine = precond_local(2, PRE2, t1_faces)
    gather_forward(2)
    w1_east, w1_south, column = precond_finish(2, PRE2, mine)
    w1 = (w1_east, w1_south)

    rz1 = column(0)
    ratio = rz1 / rz0
    step1 = rz1 / (column(1) + ratio * (column(2) + column(3)) + ratio * ratio * dq0)
    for f in range(2):
        place = slice(f * F, (f + 1) * F)
        direction = z1[f] + ratio * z0[f]
        x_ref[0, 0, :, place] = (step0 * z0[f] + step1 * direction)[:, :F]
        r_ref[0, 0, :, place] = (r1[f] - step1 * (t1[f] + ratio * q0[f]))[:, :F]
        z_ref[0, 0, :, place] = (z1[f] - step1 * (w1[f] + ratio * w0[f]))[:, :F]

    for copy in started:
        copy.wait_send()


def shards(applied_loads, bound_block, coupling, interior_inverse, local_inverse, coarse_inverse):
    out = jax.ShapeDtypeStruct((1, 1, K, 2 * F), f32)
    dma = pltpu.SemaphoreType.DMA
    return pl.pallas_call(
        kernel,
        out_shape=(out, out, out),
        in_specs=[pl.BlockSpec(memory_space=pl.ANY)] * 6,
        out_specs=tuple(pl.BlockSpec(memory_space=pltpu.VMEM) for _ in range(3)),
        scratch_shapes=[
            pltpu.VMEM((K, 2 * F), f32),
            pltpu.VMEM((NF, NF), f32),
            pltpu.VMEM((NF, NI), f32),
            pltpu.VMEM((NI, NI), f32),
            pltpu.VMEM((NF, NF), f32),
            pltpu.VMEM((32, NC), f32),
            dma((6,)),
            pltpu.VMEM((NP, NP), bf16),
            pltpu.VMEM((NP, NP), bf16),
            pltpu.VMEM((NP, NP), bf16),
            pltpu.VMEM((NP, NP), bf16),
            pltpu.VMEM((NF, NI), bf16),
            pltpu.VMEM((NF, NI), bf16),
            pltpu.VMEM((NI, COLS), bf16),
            pltpu.VMEM((NI, COLS), bf16),
            pltpu.VMEM((NF, NI), bf16),
            pltpu.VMEM((NF, NI), bf16),
            pltpu.VMEM((NF, NF), f32),
            pltpu.VMEM((2, 32, NC // 2), f32),
            pltpu.VMEM((32, NC // 2), f32),
            pltpu.VMEM((128, NC // 2), bf16),
            pltpu.VMEM((3, LZ, 8, FP), f32),
            pltpu.VMEM((3, LX * LY, 40, FP), f32),
            pltpu.VMEM((3, 24, FP), f32),
            pltpu.VMEM((3, 24, FP), f32),
            pltpu.VMEM((SLOTS, K, FP), f32),
            pltpu.VMEM((SLOTS, K, FP), f32),
            dma((3, LZ)),
            dma((3, LZ)),
            dma((3, LX * LY)),
            dma((3, LX * LY)),
            dma,
            dma,
            dma((3,)),
            dma((3,)),
            dma((SLOTS,)),
            dma((SLOTS,)),
        ],
        compiler_params=pltpu.CompilerParams(
            collective_id=0, has_side_effects=True, vmem_limit_bytes=40 * 1024 * 1024
        ),
    )(applied_loads, bound_block, coupling, interior_inverse, local_inverse, coarse_inverse)


def solution(mesh):
    blocks = P("sx", "sy", None, None)
    return jax.shard_map(
        shards,
        mesh=mesh,
        in_specs=(blocks, blocks, blocks, blocks, blocks, P(("sx", "sy"), None)),
        out_specs=(blocks, blocks, blocks),
        check_vma=False,
    )
```

time: 614 us -> 77.4 us (0.13)
  blocking collectives: 440 us -> 0 us
  Pallas kernels: 0 us -> 66.5 us
  local copies, waits for them, and re-layouts: 60.5 us -> 9.86 us
  starting transfers between devices: 50.1 us -> 0 us
  matrix products: 25 us -> 0 us
  other arithmetic: 21 us -> 0 us
  waiting for transfers between devices: 12.7 us -> 0 us
    psum x3 -> x0, blocking collectives: 233 us -> none  [the longest x2 155 us: residual_dots(): return lax.psum(local_dot(left, right), ('sx', 'sy'))]
    all_gather x3 -> x0, blocking collectives: 208 us -> none  [coarse_part(): lax.all_gather(group_sums, ('sx', 'sy'), axis=1, tiled=True)]
    pallas_call x0 -> x1, Pallas kernels: none -> 66.5 us  [shards(): pl.pallas_call(kernel, out_shape=(out, out, out), in_specs=[pl.BlockSpec(...]
    ppermute x20 -> x0, starting transfers between devices: 50.1 us -> none  [shifted(): return lax.ppermute(value, axis, pairs)]
    dot_general x14 -> x0, matrix products: 25 us -> none  [the longest x9 16.9 us: matmul(): return jnp.dot(left, right, precision=precise)]
    concatenate x10 -> x0, local copies, waits for them, and re-layouts: 13.1 us -> none  [exchange_faces(): return jnp.concatenate([east_total, south_total], axis=1)]
    ppermute x20 -> x0, waiting for transfers between devices: 12.7 us -> none  [shifted(): return lax.ppermute(value, axis, pairs)]
    add x8 -> x0, local copies, waits for them, and re-layouts: 11.2 us -> none  [owner_sums(): return (result[:, F:2 * F] + east_back, result[:, 3 * F:] + south_back)]
  transfers between devices with their start and end apart: 20 -> 0, of which waited for: 7 -> 0; matrix products, arithmetic and copies ran while one was open for 8% -> 0% of each run, Pallas kernels for 0% -> 0%
where the time goes in v1:
time: 77.4 us; the launch traced here: 77 us
  Pallas kernels  66.5 us (86%)
  local copies, waits for them, and re-layouts  9.86 us (13%)
    pallas_call x1, Pallas kernels, shards(): pl.pallas_call(kernel, out_shape=(out, out, out), in_specs=[pl.BlockSpec(...  66.5 us
    unnamed x15, local copies, waits for them, and re-layouts  9.86 us

profile of v1, /device:TPU:1, one launch (start us, length us, event | category | flops | bytes accessed | tf_op | source)
XLA Modules:
  0.0 77.0 jit_solution(8523696755579319510)
XLA Ops:
  0.6 0.0 copy-start
  0.6 2.5 %copy-done = f32[1,1,1152,1152]{3,2,1,0:T(8,128)S(1)} copy-done((f32[1,1,1152,1152]{3,2,1,0:T(8,128)S(1)}, f32[1,1,1152,1152]{3,2,1,0:T(8,128)}, u32[]{:S(2)}) %copy-start) | copy-done | bytes 5308440
  3.1 0.0 copy-start.1
  3.1 1.5 %copy-done.1 = f32[1,1,384,1152]{3,2,1,0:T(8,128)S(1)} copy-done((f32[1,1,384,1152]{3,2,1,0:T(8,128)S(1)}, f32[1,1,384,1152]{3,2,1,0:T(8,128)}, u32[]{:S(2)}) %copy-start.1) | copy-done | bytes 1769496
  4.6 0.0 copy-start.2
  4.6 1.2 %copy-done.2 = f32[32,8192]{1,0:T(8,128)S(1)} copy-done((f32[32,8192]{1,0:T(8,128)S(1)}, f32[32,8192]{1,0:T(8,128)}, u32[]{:S(2)}) %copy-start.2) | copy-done | bytes 1048600
  5.8 0.0 copy-start.3
  5.8 1.1 %copy-done.3 = f32[1,1,384,384]{3,2,1,0:T(8,128)S(1)} copy-done((f32[1,1,384,384]{3,2,1,0:T(8,128)S(1)}, f32[1,1,384,384]{3,2,1,0:T(8,128)}, u32[]{:S(2)}) %copy-start.3) | copy-done | bytes 589848
  6.9 0.0 copy-start.4
  6.9 1.1 %copy-done.4 = f32[1,1,384,384]{3,2,1,0:T(8,128)S(1)} copy-done((f32[1,1,384,384]{3,2,1,0:T(8,128)S(1)}, f32[1,1,384,384]{3,2,1,0:T(8,128)}, u32[]{:S(2)}) %copy-start.4) | copy-done | bytes 589848
  8.0 0.0 copy-start.5
  8.0 0.7 copy-done.5
  8.7 66.5 %shard_map.85 = (f32[1,1,16,192]{3,2,1,0:T(8,128)S(1)}, f32[1,1,16,192]{3,2,1,0:T(8,128)S(1)}, f32[1,1,16,192]{3,2,1,0:T(8,128)S(1)}) custom-call(f32[1,1,16,192]{3,2,1,0:T(8,128)S(1)} %copy-done.5, f32[1,1,384,384]{3,2,1,0:T(8,128)S(1)} %copy-done.3, f32[1,1,384,1152]{3,2,1,0:T(8,128)S(1)} %copy-done.1, f32[1,1,1152,1152]{3,2,1,0:T(8,128)S(1)} %copy-done, ...), custom_call_target="tpu_custom_call" | custom-call | tf_op jit(solution)/shard_map/pallas_call | solution.py:377
  75.2 0.6 copy.12
  75.8 0.6 copy.13
  76.4 0.6 copy.14
Async XLA Ops:
  0.6 2.5 %copy-start = (f32[1,1,1152,1152]{3,2,1,0:T(8,128)S(1)}, f32[1,1,1152,1152]{3,2,1,0:T(8,128)}, u32[]{:S(2)}) copy-start(f32[1,1,1152,1152]{3,2,1,0:T(8,128)} %interior_ref.1) | copy-start | bytes 15925252
  3.1 1.5 %copy-start.1 = (f32[1,1,384,1152]{3,2,1,0:T(8,128)S(1)}, f32[1,1,384,1152]{3,2,1,0:T(8,128)}, u32[]{:S(2)}) copy-start(f32[1,1,384,1152]{3,2,1,0:T(8,128)} %coupling_ref.1) | copy-start | bytes 5308420
  4.6 1.2 %copy-start.2 = (f32[32,8192]{1,0:T(8,128)S(1)}, f32[32,8192]{1,0:T(8,128)}, u32[]{:S(2)}) copy-start(f32[32,8192]{1,0:T(8,128)} %coarse_ref.1) | copy-start | bytes 3145732
  5.8 1.1 %copy-start.3 = (f32[1,1,384,384]{3,2,1,0:T(8,128)S(1)}, f32[1,1,384,384]{3,2,1,0:T(8,128)}, u32[]{:S(2)}) copy-start(f32[1,1,384,384]{3,2,1,0:T(8,128)} %bound_ref.1) | copy-start | bytes 1769476
  6.9 1.1 %copy-start.4 = (f32[1,1,384,384]{3,2,1,0:T(8,128)S(1)}, f32[1,1,384,384]{3,2,1,0:T(8,128)}, u32[]{:S(2)}) copy-start(f32[1,1,384,384]{3,2,1,0:T(8,128)} %local_ref.1) | copy-start | bytes 1769476
  8.0 0.7 copy-start.5

commit v2 on v1

v2 whole, which is shorter than its diff:
```python
import jax
import jax.numpy as jnp
from jax import lax
from jax.experimental import pallas as pl
from jax.experimental.pallas import tpu as pltpu
from jax.sharding import PartitionSpec as P

MESH = pl.DeviceIdType.MESH
F = 96
FP = 128
FACES = 4
K = 16
NF = FACES * F
NP = FACES * FP
NI = 1152
NC = 8192
LX, LY, LZ = 4, 4, 8
COLS = 384
PLANE_ORDER = sorted(range(LX * LY), key=lambda s: min(s // LX, LY - s // LX) + min(s % LX, LX - s % LX))
f32, bf16 = jnp.float32, jnp.bfloat16

LOADS_W, LOADS_N = 0, 1
PRE0, PRE1, PRE2 = 2, 6, 10
SCH0, SCH1 = 12, 16
SLOTS = 20


def split(value):
    high = value.astype(bf16)
    low = (value - high.astype(f32)).astype(bf16)
    return high, low


def dot(left, right):
    return jnp.dot(left, right, preferred_element_type=f32)


def dot_t(left, right):
    return lax.dot_general(left, right, (((1,), (1,)), ((), ())), preferred_element_type=f32)


def pad_split(get_block, high_ref, low_ref):
    high_ref[...] = jnp.zeros_like(high_ref)
    low_ref[...] = jnp.zeros_like(low_ref)
    for a in range(FACES):
        for b in range(FACES):
            high, low = split(get_block(a, b))
            high_ref[a * FP : a * FP + F, b * FP : b * FP + F] = high
            low_ref[a * FP : a * FP + F, b * FP : b * FP + F] = low


def apply_local(faces, high_ref, low_ref):
    high, low = split(jnp.concatenate(faces, axis=1))
    both = dot(jnp.concatenate([high, low], axis=0), high_ref[...])
    result = both[:K] + both[K:] + dot(high, low_ref[...])
    return [result[:, f * FP : (f + 1) * FP] for f in range(FACES)]


def kernel(
    loads_ref, bound_ref, coupling_ref, interior_ref, local_ref, coarse_ref,
    out_ref,
    loads_v, bound_v, coupling_v, interior_v, local_v, coarse_v, load_sem,
    l_high, l_low, s_high, s_low, c_high, c_low, i_high, i_low, t_high, t_low, schur_v,
    permuted, partner_rows, coarse_w, restrict_v, spread_v,
    line_v, west_out, west_in, head_in, plane_v, part_out, part_in, halo_out, halo_in,
    line_send, line_recv, west_send, west_recv, head_send, head_recv, plane_send, plane_recv,
    swap_send, swap_recv, part_send, part_recv, halo_send, halo_recv,
):
    i = lax.axis_index("sx")
    j = lax.axis_index("sy")
    y, z = lax.div(i, LZ), lax.rem(i, LZ)
    x, core = lax.div(j, 2), lax.rem(j, 2)
    block = y * LX + x
    east = {"sx": i, "sy": lax.rem(j + 1, 2 * LX)}
    west = {"sx": i, "sy": lax.rem(j + 2 * LX - 1, 2 * LX)}
    south = {"sx": lax.rem(i + 1, LY * LZ), "sy": j}
    north = {"sx": lax.rem(i + LY * LZ - 1, LY * LZ), "sy": j}
    partner = {"sx": i, "sy": x * 2 + (1 - core)}
    line = [{"sx": y * LZ + lax.rem(z + s, LZ), "sy": j} for s in range(LZ)]
    west_line = [{"sx": device["sx"], "sy": west["sy"]} for device in line]
    east_line = [{"sx": device["sx"], "sy": east["sy"]} for device in line]
    north_line = [{"sx": lax.rem(y + LY - 1, LY) * LZ + s, "sy": j} for s in range(LZ)]
    south_head = {"sx": lax.rem(y + 1, LY) * LZ, "sy": j}
    plane = [
        {"sx": lax.rem(y + s // LX, LY) * LZ + z, "sy": lax.rem(x + s % LX, LX) * 2 + core} for s in range(LX * LY)
    ]
    south_pair = [south, {"sx": south["sx"], "sy": partner["sy"]}]
    east_pair = [{"sx": i, "sy": lax.rem(x + 1, LX) * 2 + core}, {"sx": i, "sy": lax.rem(x + 1, LX) * 2 + 1 - core}]
    north_other = {"sx": north["sx"], "sy": partner["sy"]}
    west_other = {"sx": i, "sy": lax.rem(x + LX - 1, LX) * 2 + 1 - core}

    barrier = pltpu.get_barrier_semaphore()
    greeted = [east, west, south, north, partner, north_other, west_other, south_head]
    greeted += line[1:] + plane[1:] + east_line
    for device in greeted:
        pl.semaphore_signal(barrier, 1, device_id=device, device_id_type=MESH)

    fetches = [
        pltpu.make_async_copy(source, target, load_sem.at[k])
        for k, (source, target) in enumerate(
            [
                (loads_ref.at[0, 0], loads_v),
                (coarse_ref, coarse_v),
                (coupling_ref.at[0, 0], coupling_v),
                (interior_ref.at[0, 0], interior_v),
                (local_ref.at[0, 0], local_v),
                (bound_ref.at[0, 0], bound_v),
            ]
        )
    ]
    for fetch in fetches:
        fetch.start()

    has_west, has_east = j > 0, j < 2 * LX - 1
    has_north, has_south = i > 0, i < LY * LZ - 1

    def halo_copy(slot, device):
        return pltpu.make_async_remote_copy(
            halo_out.at[slot], halo_in.at[slot], halo_send.at[slot], halo_recv.at[slot], device_id=device, device_id_type=MESH
        )

    def halo_start(slot, device, value):
        halo_out[slot] = value
        copy = halo_copy(slot, device)
        copy.start()
        started.append(copy)

    def halo_wait(slot, device, present):
        halo_copy(slot, device).wait_recv()
        return jnp.where(present, halo_in[slot], 0.0)

    started = []

    lane_row = lax.broadcasted_iota(jnp.int32, (1, FP), 1)
    lane_group = lane_row // 32
    south_lanes = lane_row % 32 >= 16
    case = lax.broadcasted_iota(jnp.int32, (K, FP), 0)
    lane = lax.broadcasted_iota(jnp.int32, (K, FP), 1)
    value_lane = lax.broadcasted_iota(jnp.int32, (2 * FP, FP), 0)
    coarse_lane = lax.broadcasted_iota(jnp.int32, (2 * FP, FP), 1) % 32
    in_face = value_lane % FP
    run_of = (value_lane // FP) * 16 + in_face // 6
    restrict_v[...] = ((run_of == coarse_lane) & (in_face < F)).astype(f32).astype(bf16)
    coarse_at = lax.broadcasted_iota(jnp.int32, (FP, 3 * FP), 0) % 64
    value_at = lax.broadcasted_iota(jnp.int32, (FP, 3 * FP), 1)
    value_in = value_at % FP
    face_at = value_at // FP
    first = jnp.where(face_at == 2, (1 - core) * 32, core * 32 + face_at * 16)
    spread_v[...] = ((first + value_in // 6 == coarse_at) & (value_in < F)).astype(f32).astype(bf16)

    def line_copy(phase, s):
        return pltpu.make_async_remote_copy(
            line_v.at[phase, z], line_v.at[phase, z], line_send.at[phase, s], line_recv.at[phase, s],
            device_id=line[s], device_id_type=MESH,
        )

    def west_copy(phase, s):
        return pltpu.make_async_remote_copy(
            west_out.at[phase], west_in.at[phase, z], west_send.at[phase, s], west_recv.at[phase, s],
            device_id=west_line[s], device_id_type=MESH,
        )

    def head_copy(phase, s):
        return pltpu.make_async_remote_copy(
            line_v.at[phase, z], head_in.at[phase], head_send.at[phase, s], head_recv.at[phase],
            device_id=north_line[s], device_id_type=MESH,
        )

    def plane_copy(phase, s):
        return pltpu.make_async_remote_copy(
            plane_v.at[phase, block], plane_v.at[phase, block], plane_send.at[phase, s], plane_recv.at[phase, s],
            device_id=plane[s], device_id_type=MESH,
        )

    def part_copy(phase, k, slot, device):
        return pltpu.make_async_remote_copy(
            part_out.at[phase], part_in.at[phase, slot], part_send.at[phase, k], part_recv.at[phase, slot],
            device_id=device, device_id_type=MESH,
        )

    def go(copy):
        copy.start()
        started.append(copy)

    def pack(sums):
        packed = sums[:4]
        for q in range(1, 4):
            packed = jnp.where(lane_group == q, sums[4 * q : 4 * q + 4], packed)
        return packed

    def gather_start(phase, own, shared, dots):
        values = [jnp.concatenate(own, axis=1)] + ([jnp.concatenate(shared, axis=1)] if shared else [])
        high, low = split(jnp.concatenate(values, axis=0))
        rows = len(values) * K
        sums = dot(jnp.concatenate([high, low], axis=0), restrict_v[...])
        sums = sums[:rows] + sums[rows:]
        line_v[phase, z, :4] = pack(sums[:K])
        if not shared:
            line_v[phase, z, 4:] = jnp.zeros((4, FP), f32)
        else:
            others = pack(sums[K:])
            west_out[phase] = others
            for s in range(LZ):
                go(west_copy(phase, s))
            placed = jnp.zeros((K, FP), f32)
            for d, (left, right) in enumerate(dots):
                product = left[0] * right[0]
                for f in range(1, len(left)):
                    product += left[f] * right[f]
                placed = jnp.where(lane == d * 32 + case, jnp.sum(product, axis=1, keepdims=True), placed)
            row = jnp.sum(placed, axis=0, keepdims=True)
            line_v[phase, z, 4:] = jnp.where(south_lanes, others, row)

            @pl.when(z == 0)
            def _():
                for s in range(LZ):
                    head_copy(phase, s).start()

        for s in range(1, LZ):
            go(line_copy(phase, s))

    def gather_forward(phase, shared):
        for s in range(1, LZ):
            line_copy(phase, s).wait_recv()
        if shared:
            for s in range(LZ):
                west_copy(phase, s).wait_recv()
            head_copy(phase, 0).wait_recv()
        tiles = []
        for s in range(LZ):
            tile = line_v[phase, s, :4]
            if shared:
                if s + 1 < LZ:
                    below = line_v[phase, s + 1, 4:]
                else:
                    below = jnp.where(y < LY - 1, head_in[phase, 4:], 0.0)
                right = jnp.where(has_east, west_in[phase, s], 0.0)
                tile = tile + jnp.where(south_lanes, below, right)
            tiles.append(tile)
        for h in range(2):
            rows = []
            for q in range(4):
                mixed = None
                for d in range(4):
                    turn = ((d - q) % 4) * 32
                    tile = tiles[4 * h + d]
                    turned = pltpu.roll(tile, turn, 1) if turn else tile
                    mixed = turned if mixed is None else jnp.where(lane_group == d, turned, mixed)
                rows.append(mixed)
            plane_v[phase, block, h * K : (h + 1) * K] = jnp.concatenate(rows, axis=0)
        total = line_v[phase, 0]
        for s in range(1, LZ):
            total = total + line_v[phase, s]
        plane_v[phase, block, 2 * K :] = total
        for s in PLANE_ORDER[1:]:
            go(plane_copy(phase, s))

    def gather_finish(phase, last):
        total = jnp.zeros((2 * K, FP), f32)
        sums = jnp.zeros((8, FP), f32)
        for s in PLANE_ORDER:
            if s:
                plane_copy(phase, s).wait_recv()
            b = lax.rem(y + LY - s // LX, LY) * LX + lax.rem(x + LX - s % LX, LX)
            value = jnp.concatenate([plane_v[phase, b, :K], plane_v[phase, b, K : 2 * K]], axis=1)
            high, low = split(value)
            total += dot_t(jnp.concatenate([high, low], axis=0), coarse_w[b])
            sums += plane_v[phase, b, 2 * K :]
        part = total[:K] + total[K:]
        part_out[phase, :K] = part
        part_out[phase, K:] = sums
        if not last:
            for k in range(2):
                go(part_copy(phase, k, 1 + core, south_pair[k]))
                go(part_copy(phase, 2 + k, 3 + core, east_pair[k]))
        go(part_copy(phase, 4, 0, partner))
        part_copy(phase, 4, 0, partner).wait_recv()
        own = part + part_in[phase, 0, :K]
        sums = sums + part_in[phase, 0, K:]

        def column(d):
            return jnp.sum(jnp.where(lane == d * 32 + case, sums[4:5], 0.0), axis=1, keepdims=True)

        groups = [own]
        if not last:
            for slot in range(1, 5):
                part_copy(phase, 0, slot, partner).wait_recv()
            groups.append(part_in[phase, 1, :K] + part_in[phase, 2, :K])
            groups.append(jnp.where(core == 0, part_in[phase, 3, :K] + part_in[phase, 4, :K], own))
        high, low = split(jnp.concatenate(groups, axis=0))
        rows = len(groups) * K
        wide = dot(jnp.concatenate([high, low], axis=0), spread_v[...])
        wide = wide[:rows] + wide[rows:]
        faces = [wide[:K, :FP], wide[:K, FP : 2 * FP]]
        if not last:
            faces = [wide[2 * K :, 2 * FP :], faces[0], wide[K : 2 * K, FP : 2 * FP], faces[1]]
        return faces, column

    def spread_faces(slot, result, last=False):
        halo_start(slot, west, result[0])
        halo_start(slot + 1, north, result[2])
        if not last:
            halo_start(slot + 2, east, result[1])
            halo_start(slot + 3, south, result[3])

    def total_faces(slot, result, last=False):
        east_total = result[1] + halo_wait(slot, west, has_east)
        south_total = result[3] + halo_wait(slot + 1, north, has_south)
        if last:
            return [east_total, south_total]
        west_total = result[0] + halo_wait(slot + 2, east, has_west)
        north_total = result[2] + halo_wait(slot + 3, south, has_north)
        return inner_faces([west_total, east_total, north_total, south_total])

    def inner_faces(faces):
        return [jnp.where(has_west, faces[0], 0.0), faces[1], jnp.where(has_north, faces[2], 0.0), faces[3]]

    def owned(faces):
        return [faces[1], faces[3]]

    fetches[0].wait()
    padding = jnp.zeros((K, FP - F), f32)
    r0 = [
        jnp.concatenate([loads_v[:, :F], padding], axis=1),
        jnp.concatenate([loads_v[:, F : 2 * F], padding], axis=1),
    ]

    fetches[1].wait()

    def permute(step, _):
        y_at, rest = lax.div(step, 4), lax.rem(step, 4)
        half, j_half = lax.div(rest, 2), lax.rem(rest, 2)
        tiles = []
        for d in range(4):
            at = ((y_at * LZ + half * 4 + d) * 2 + j_half) * FP
            tiles.append(coarse_v[:, pl.ds(pl.multiple_of(at, FP), FP)])
        for q in range(4):
            mixed = tiles[q] if q == 0 else pltpu.roll(tiles[0], ((0 - q) % 4) * 32, 1)
            for d in range(1, 4):
                turn = ((d - q) % 4) * 32
                turned = pltpu.roll(tiles[d], turn, 1) if turn else tiles[d]
                mixed = jnp.where(lane_group == d, turned, mixed)
            at = (y_at * LX + j_half * 2 + q // 2) * 256 + half * FP
            permuted[q % 2, :, pl.ds(pl.multiple_of(at, FP), FP)] = mixed
        return 0

    lax.fori_loop(0, 16, permute, 0)
    fetches[2].wait()
    c_high[...], c_low[...] = split(coupling_v[...])

    pl.semaphore_wait(barrier, len(greeted) - 1 + LZ * lax.div(LZ - 1 - z, LZ - 1))

    gather_start(0, r0, None, None)
    halo_start(LOADS_W, east, r0[0])
    halo_start(LOADS_N, south, r0[1])
    swap = pltpu.make_async_remote_copy(
        permuted.at[1 - core], partner_rows, swap_send, swap_recv, device_id=partner, device_id_type=MESH
    )
    go(swap)

    def times_interior(step, _):
        columns = pl.ds(pl.multiple_of(step * COLS, FP), COLS)
        i_high[...], i_low[...] = split(interior_v[:, columns])
        total = dot(c_high[...], i_high[...]) + dot(c_low[...], i_high[...]) + dot(c_high[...], i_low[...])
        t_high[:, columns], t_low[:, columns] = split(total)
        return 0

    fetches[3].wait()
    lax.fori_loop(0, 1, times_interior, 0)

    fetches[4].wait()
    pad_split(lambda a, b: local_v[a * F : (a + 1) * F, b * F : (b + 1) * F], l_high, l_low)
    from_west = halo_wait(LOADS_W, east, has_west)
    from_north = halo_wait(LOADS_N, south, has_north)
    z0_local = apply_local([from_west, r0[0], from_north, r0[1]], l_high, l_low)
    spread_faces(PRE0, z0_local)

    gather_forward(0, False)

    def place_rows(value, at):
        high, low = split(value)
        for b in range(LX * LY):
            coarse_w[b, pl.ds(pl.multiple_of(at, 32), 32)] = high[:, b * 256 : (b + 1) * 256]
            coarse_w[b, pl.ds(pl.multiple_of(64 + at, 32), 32)] = low[:, b * 256 : (b + 1) * 256]

    place_rows(permuted[core], core * 32)
    swap.wait_recv()
    place_rows(partner_rows[...], (1 - core) * 32)
    lax.fori_loop(1, NI // COLS, times_interior, 0)
    back = dot_t(t_high[...], c_high[...]) + dot_t(t_low[...], c_high[...]) + dot_t(t_high[...], c_low[...])
    fetches[5].wait()
    schur_v[...] = bound_v[...] - back
    pad_split(lambda a, b: schur_v[a * F : (a + 1) * F, b * F : (b + 1) * F], s_high, s_low)

    z0_local = total_faces(PRE0, z0_local)
    wide, _ = gather_finish(0, False)
    z0 = inner_faces([a + b for a, b in zip(z0_local, wide)])

    image = apply_local(z0, s_high, s_low)
    gather_start(1, owned(image), [image[0], image[2]], [(r0, owned(z0)), (z0, image)])
    spread_faces(SCH0, image)
    q0_faces = total_faces(SCH0, image)
    w0_local = apply_local(q0_faces, l_high, l_low)
    spread_faces(PRE1, w0_local)
    gather_forward(1, True)
    w0_local = total_faces(PRE1, w0_local)
    wide, column = gather_finish(1, False)
    rz0, dq0 = column(0), column(1)
    step0 = rz0 / dq0
    w0 = [a + b for a, b in zip(w0_local, wide)]
    z1 = inner_faces([a - step0 * b for a, b in zip(z0, w0)])

    image = apply_local(z1, s_high, s_low)
    q0, z0_own, z1_own = owned(q0_faces), owned(z0), owned(z1)
    r1 = [a - step0 * b for a, b in zip(r0, q0)]
    gather_start(2, owned(image), [image[0], image[2]], [(r1, z1_own), (z1, image), (z0, image), (z1_own, q0)])
    spread_faces(SCH1, image)
    t1_faces = total_faces(SCH1, image)
    w1_local = apply_local(t1_faces, l_high, l_low)
    spread_faces(PRE2, w1_local, True)
    gather_forward(2, True)
    w1_local = total_faces(PRE2, w1_local, True)
    wide, column = gather_finish(2, True)
    w1 = [a + b for a, b in zip(w1_local, wide)]

    t1, w0 = owned(t1_faces), owned(w0)
    rz1 = column(0)
    ratio = rz1 / rz0
    step1 = rz1 / (column(1) + ratio * (column(2) + column(3)) + ratio * ratio * dq0)
    for f in range(2):
        place = slice(f * FP, (f + 1) * FP)
        direction = z1_own[f] + ratio * z0_own[f]
        out_ref[0, :, place] = step0 * z0_own[f] + step1 * direction
        out_ref[1, :, place] = r1[f] - step1 * (t1[f] + ratio * q0[f])
        out_ref[2, :, place] = z1_own[f] - step1 * (w1[f] + ratio * w0[f])

    for copy in started:
        copy.wait_send()

    @pl.when(z == 0)
    def _():
        for phase in range(1, 3):
            for s in range(LZ):
                head_copy(phase, s).wait_send()


def unpad(packed_ref, *out_refs):
    for k, out_ref in enumerate(out_refs):
        out_ref[0, 0, :, :F] = packed_ref[k, :, :F]
        out_ref[0, 0, :, F:] = packed_ref[k, :, FP : FP + F]


def shards(applied_loads, bound_block, coupling, interior_inverse, local_inverse, coarse_inverse):
    dma = pltpu.SemaphoreType.DMA
    packed = pl.pallas_call(
        kernel,
        out_shape=jax.ShapeDtypeStruct((3, K, 2 * FP), f32),
        in_specs=[pl.BlockSpec(memory_space=pltpu.HBM)] * 6,
        out_specs=pl.BlockSpec(memory_space=pltpu.VMEM),
        scratch_shapes=[
            pltpu.VMEM((K, 2 * F), f32),
            pltpu.VMEM((NF, NF), f32),
            pltpu.VMEM((NF, NI), f32),
            pltpu.VMEM((NI, NI), f32),
            pltpu.VMEM((NF, NF), f32),
            pltpu.VMEM((32, NC), f32),
            dma((6,)),
            pltpu.VMEM((NP, NP), bf16),
            pltpu.VMEM((NP, NP), bf16),
            pltpu.VMEM((NP, NP), bf16),
            pltpu.VMEM((NP, NP), bf16),
            pltpu.VMEM((NF, NI), bf16),
            pltpu.VMEM((NF, NI), bf16),
            pltpu.VMEM((NI, COLS), bf16),
            pltpu.VMEM((NI, COLS), bf16),
            pltpu.VMEM((NF, NI), bf16),
            pltpu.VMEM((NF, NI), bf16),
            pltpu.VMEM((NF, NF), f32),
            pltpu.VMEM((2, 32, NC // 2), f32),
            pltpu.VMEM((32, NC // 2), f32),
            pltpu.VMEM((LX * LY, 128, 256), bf16),
            pltpu.VMEM((2 * FP, FP), bf16),
            pltpu.VMEM((FP, 3 * FP), bf16),
            pltpu.VMEM((3, LZ, 8, FP), f32),
            pltpu.VMEM((3, 4, FP), f32),
            pltpu.VMEM((3, LZ, 4, FP), f32),
            pltpu.VMEM((3, 8, FP), f32),
            pltpu.VMEM((3, LX * LY, 40, FP), f32),
            pltpu.VMEM((3, 24, FP), f32),
            pltpu.VMEM((3, 5, 24, FP), f32),
            pltpu.VMEM((SLOTS, K, FP), f32),
            pltpu.VMEM((SLOTS, K, FP), f32),
            dma((3, LZ)),
            dma((3, LZ)),
            dma((3, LZ)),
            dma((3, LZ)),
            dma((3, LZ)),
            dma((3,)),
            dma((3, LX * LY)),
            dma((3, LX * LY)),
            dma,
            dma,
            dma((3, 5)),
            dma((3, 5)),
            dma((SLOTS,)),
            dma((SLOTS,)),
        ],
        compiler_params=pltpu.CompilerParams(
            collective_id=0, has_side_effects=True, vmem_limit_bytes=60 * 1024 * 1024
        ),
    )(applied_loads, bound_block, coupling, interior_inverse, local_inverse, coarse_inverse)
    out = jax.ShapeDtypeStruct((1, 1, K, 2 * F), f32)
    return pl.pallas_call(unpad, out_shape=(out, out, out))(packed)


def solution(mesh):
    blocks = P("sx", "sy", None, None)
    return jax.shard_map(
        shards,
        mesh=mesh,
        in_specs=(blocks, blocks, blocks, blocks, blocks, P(("sx", "sy"), None)),
        out_specs=(blocks, blocks, blocks),
        check_vma=False,
    )
```

time: 77.4 us -> 63.6 us (0.82)
  local copies, waits for them, and re-layouts: 9.86 us -> 0 us
  Pallas kernels: 66.5 us -> 62.8 us
    unnamed x15 -> x0, local copies, waits for them, and re-layouts: 9.86 us -> none
    pallas_call x1 -> x2, Pallas kernels: 66.5 us -> 62.8 us  [the longest x1 61.3 us: shards(): pl.pallas_call(kernel, out_shape=jax.ShapeDtypeStruct((3, K, 2 * FP), f32...]
where the time goes in v2:
time: 63.6 us; the launch traced here: 63.4 us
  Pallas kernels  62.8 us (99%)
  between operations  0.64 us (1%)
    pallas_call x1, Pallas kernels, shards(): pl.pallas_call(kernel, out_shape=jax.ShapeDtypeStruct((3, K, 2 * FP), f32...  61.3 us
    pallas_call x1, Pallas kernels, shards(): return pl.pallas_call(unpad, out_shape=(out, out, out))(packed)  1.49 us

profile of v2, /device:TPU:1, one launch (start us, length us, event | category | flops | bytes accessed | tf_op | source)
XLA Modules:
  0.0 63.4 jit_solution(13432107248038807541)
XLA Ops:
  0.6 61.3 %shard_map.85.packed_ref = f32[3,16,256]{2,1,0:T(8,128)} custom-call(f32[1,1,16,192]{3,2,1,0:T(8,128)} %loads_ref.1, f32[1,1,384,384]{3,2,1,0:T(8,128)} %bound_ref.1, f32[1,1,384,1152]{3,2,1,0:T(8,128)} %coupling_ref.1, f32[1,1,1152,1152]{3,2,1,0:T(8,128)} %interior_ref.1, f32[1,1,384,384]{3,2,1,0:T(8,128)} %local_ref.1, f32[32,8192]{1,0:T(8,128)} %coarse_ref.1), custom_call_target="tpu_custom_call" | custom-call | tf_op jit(solution)/shard_map/pallas_call | solution.py:455
  62.0 1.5 %shard_map.86 = (f32[1,1,16,192]{3,2,1,0:T(8,128)}, f32[1,1,16,192]{3,2,1,0:T(8,128)}, f32[1,1,16,192]{3,2,1,0:T(8,128)}) custom-call(f32[3,16,256]{2,1,0:T(8,128)} %shard_map.85.packed_ref), custom_call_target="tpu_custom_call" | custom-call | tf_op jit(solution)/shard_map/pallas_call | solution.py:513

commit v3 on v2

--- a/solution.py
+++ b/solution.py
@@ -15,7 +15,8 @@
 NI = 1152
 NC = 8192
 LX, LY, LZ = 4, 4, 8
-COLS = 384
+COLS = 256
+LINE_ORDER = sorted(range(LZ), key=lambda s: min(s, LZ - s))
 PLANE_ORDER = sorted(range(LX * LY), key=lambda s: min(s // LX, LY - s // LX) + min(s % LX, LX - s % LX))
 f32, bf16 = jnp.float32, jnp.bfloat16
 
@@ -37,6 +38,17 @@
 
 def dot_t(left, right):
     return lax.dot_general(left, right, (((1,), (1,)), ((), ())), preferred_element_type=f32)
+
+
+def transpose_groups(tiles, lane_group):
+    a, b, c, d = tiles
+    near = lane_group < 2
+    a, c = jnp.where(near, a, pltpu.roll(c, 64, 1)), jnp.where(near, pltpu.roll(a, 64, 1), c)
+    b, d = jnp.where(near, b, pltpu.roll(d, 64, 1)), jnp.where(near, pltpu.roll(b, 64, 1), d)
+    even = lane_group % 2 == 0
+    a, b = jnp.where(even, a, pltpu.roll(b, 32, 1)), jnp.where(even, pltpu.roll(a, 96, 1), b)
+    c, d = jnp.where(even, c, pltpu.roll(d, 32, 1)), jnp.where(even, pltpu.roll(c, 96, 1), d)
+    return a, b, c, d
 
 
 def pad_split(get_block, high_ref, low_ref):
@@ -60,7 +72,7 @@
     loads_ref, bound_ref, coupling_ref, interior_ref, local_ref, coarse_ref,
     out_ref,
     loads_v, bound_v, coupling_v, interior_v, local_v, coarse_v, load_sem,
-    l_high, l_low, s_high, s_low, c_high, c_low, i_high, i_low, t_high, t_low, schur_v,
+    l_high, l_low, s_high, s_low, c_parts, t_parts, schur_v,
     permuted, partner_rows, coarse_w, restrict_v, spread_v,
     line_v, west_out, west_in, head_in, plane_v, part_out, part_in, halo_out, halo_in,
     line_send, line_recv, west_send, west_recv, head_send, head_recv, plane_send, plane_recv,
@@ -89,12 +101,6 @@
     north_other = {"sx": north["sx"], "sy": partner["sy"]}
     west_other = {"sx": i, "sy": lax.rem(x + LX - 1, LX) * 2 + 1 - core}
 
-    barrier = pltpu.get_barrier_semaphore()
-    greeted = [east, west, south, north, partner, north_other, west_other, south_head]
-    greeted += line[1:] + plane[1:] + east_line
-    for device in greeted:
-        pl.semaphore_signal(barrier, 1, device_id=device, device_id_type=MESH)
-
     fetches = [
         pltpu.make_async_copy(source, target, load_sem.at[k])
         for k, (source, target) in enumerate(
@@ -108,7 +114,16 @@
             ]
         )
     ]
-    for fetch in fetches:
+    fetches[0].start()
+
+    barrier = pltpu.get_barrier_semaphore()
+    greeted = [device for s in LINE_ORDER[:0:-1] for device in (east_line[s], line[s])]
+    greeted += [plane[s] for s in PLANE_ORDER[:0:-1]]
+    greeted += [south_head, north_other, west_other, north, south, east_line[0], east, west, partner]
+    for device in greeted:
+        pl.semaphore_signal(barrier, 1, device_id=device, device_id_type=MESH)
+
+    for fetch in fetches[1:]:
         fetch.start()
 
     has_west, has_east = j > 0, j < 2 * LX - 1
@@ -141,7 +156,7 @@
     in_face = value_lane % FP
     run_of = (value_lane // FP) * 16 + in_face // 6
     restrict_v[...] = ((run_of == coarse_lane) & (in_face < F)).astype(f32).astype(bf16)
-    coarse_at = lax.broadcasted_iota(jnp.int32, (FP, 3 * FP), 0) % 64
+    coarse_at = lax.broadcasted_iota(jnp.int32, (FP, 3 * FP), 0)
     value_at = lax.broadcasted_iota(jnp.int32, (FP, 3 * FP), 1)
     value_in = value_at % FP
     face_at = value_at // FP
@@ -167,14 +182,16 @@
         )
 
     def plane_copy(phase, s):
+        rows = pl.ds(0, 40 if phase else 32)
         return pltpu.make_async_remote_copy(
-            plane_v.at[phase, block], plane_v.at[phase, block], plane_send.at[phase, s], plane_recv.at[phase, s],
+            plane_v.at[phase, block, rows], plane_v.at[phase, block, rows], plane_send.at[phase, s], plane_recv.at[phase, s],
             device_id=plane[s], device_id_type=MESH,
         )
 
     def part_copy(phase, k, slot, device):
+        rows = pl.ds(0, 16 if k == 4 else 8)
         return pltpu.make_async_remote_copy(
-            part_out.at[phase], part_in.at[phase, slot], part_send.at[phase, k], part_recv.at[phase, slot],
+            part_out.at[phase, rows], part_in.at[phase, slot, rows], part_send.at[phase, k], part_recv.at[phase, slot],
             device_id=device, device_id_type=MESH,
         )
 
@@ -200,7 +217,7 @@
         else:
             others = pack(sums[K:])
             west_out[phase] = others
-            for s in range(LZ):
+            for s in LINE_ORDER[::-1]:
                 go(west_copy(phase, s))
             placed = jnp.zeros((K, FP), f32)
             for d, (left, right) in enumerate(dots):
@@ -216,7 +233,7 @@
                 for s in range(LZ):
                     head_copy(phase, s).start()
 
-        for s in range(1, LZ):
+        for s in LINE_ORDER[:0:-1]:
             go(line_copy(phase, s))
 
     def gather_forward(phase, shared):
@@ -237,64 +254,64 @@
                 right = jnp.where(has_east, west_in[phase, s], 0.0)
                 tile = tile + jnp.where(south_lanes, below, right)
             tiles.append(tile)
-        for h in range(2):
-            rows = []
-            for q in range(4):
-                mixed = None
-                for d in range(4):
-                    turn = ((d - q) % 4) * 32
-                    tile = tiles[4 * h + d]
-                    turned = pltpu.roll(tile, turn, 1) if turn else tile
-                    mixed = turned if mixed is None else jnp.where(lane_group == d, turned, mixed)
-                rows.append(mixed)
-            plane_v[phase, block, h * K : (h + 1) * K] = jnp.concatenate(rows, axis=0)
-        total = line_v[phase, 0]
-        for s in range(1, LZ):
-            total = total + line_v[phase, s]
-        plane_v[phase, block, 2 * K :] = total
-        for s in PLANE_ORDER[1:]:
+        pairs = [jnp.concatenate([tiles[d], tiles[4 + d]], axis=0) for d in range(4)]
+        for q, mixed in enumerate(transpose_groups(pairs, lane_group)):
+            plane_v[phase, block, 4 * q : 4 * q + 4] = mixed[:4]
+            plane_v[phase, block, K + 4 * q : K + 4 * q + 4] = mixed[4:]
+        if shared:
+            total = line_v[phase, 0]
+            for s in range(1, LZ):
+                total = total + line_v[phase, s]
+            plane_v[phase, block, 2 * K :] = total
+        for s in PLANE_ORDER[:0:-1]:
             go(plane_copy(phase, s))
 
-    def gather_finish(phase, last):
+    def gather_finish(phase, last, scalars=None):
         total = jnp.zeros((2 * K, FP), f32)
         sums = jnp.zeros((8, FP), f32)
-        for s in PLANE_ORDER:
-            if s:
-                plane_copy(phase, s).wait_recv()
-            b = lax.rem(y + LY - s // LX, LY) * LX + lax.rem(x + LX - s % LX, LX)
-            value = jnp.concatenate([plane_v[phase, b, :K], plane_v[phase, b, K : 2 * K]], axis=1)
-            high, low = split(value)
-            total += dot_t(jnp.concatenate([high, low], axis=0), coarse_w[b])
-            sums += plane_v[phase, b, 2 * K :]
+        for group in (PLANE_ORDER[:11], PLANE_ORDER[11:]):
+            for s in group:
+                if s:
+                    plane_copy(phase, s).wait_recv()
+            for s in group:
+                b = lax.rem(y + LY - s // LX, LY) * LX + lax.rem(x + LX - s % LX, LX)
+                value = jnp.concatenate([plane_v[phase, b, :K], plane_v[phase, b, K : 2 * K]], axis=1)
+                high, low = split(value)
+                total += dot_t(jnp.concatenate([high, low], axis=0), coarse_w[b])
+                if phase:
+                    sums += plane_v[phase, b, 2 * K :]
         part = total[:K] + total[K:]
-        part_out[phase, :K] = part
-        part_out[phase, K:] = sums
+        part = part + pltpu.roll(part, 64, 1)
+        part = jnp.where(lane_row < 64, part[:8], part[8:])
+        part_out[phase, :8] = part
+        part_out[phase, 8:] = sums
         if not last:
             for k in range(2):
                 go(part_copy(phase, k, 1 + core, south_pair[k]))
                 go(part_copy(phase, 2 + k, 3 + core, east_pair[k]))
         go(part_copy(phase, 4, 0, partner))
         part_copy(phase, 4, 0, partner).wait_recv()
-        own = part + part_in[phase, 0, :K]
-        sums = sums + part_in[phase, 0, K:]
+        own = part + part_in[phase, 0, :8]
+        sums = sums + part_in[phase, 0, 8:]
 
         def column(d):
             return jnp.sum(jnp.where(lane == d * 32 + case, sums[4:5], 0.0), axis=1, keepdims=True)
 
+        values = scalars(column) if scalars else None
         groups = [own]
         if not last:
             for slot in range(1, 5):
                 part_copy(phase, 0, slot, partner).wait_recv()
-            groups.append(part_in[phase, 1, :K] + part_in[phase, 2, :K])
-            groups.append(jnp.where(core == 0, part_in[phase, 3, :K] + part_in[phase, 4, :K], own))
-        high, low = split(jnp.concatenate(groups, axis=0))
+            groups.append(part_in[phase, 1, :8] + part_in[phase, 2, :8])
+            groups.append(jnp.where(core == 0, part_in[phase, 3, :8] + part_in[phase, 4, :8], own))
+        high, low = split(jnp.concatenate([half for t in groups for half in (t, pltpu.roll(t, 64, 1))], axis=0))
         rows = len(groups) * K
         wide = dot(jnp.concatenate([high, low], axis=0), spread_v[...])
         wide = wide[:rows] + wide[rows:]
         faces = [wide[:K, :FP], wide[:K, FP : 2 * FP]]
         if not last:
             faces = [wide[2 * K :, 2 * FP :], faces[0], wide[K : 2 * K, FP : 2 * FP], faces[1]]
-        return faces, column
+        return faces, values
 
     def spread_faces(slot, result, last=False):
         halo_start(slot, west, result[0])
@@ -325,6 +342,12 @@
         jnp.concatenate([loads_v[:, F : 2 * F], padding], axis=1),
     ]
 
+    pl.semaphore_wait(barrier, len(greeted) - 1 + LZ * lax.div(LZ - 1 - z, LZ - 1))
+
+    gather_start(0, r0, None, None)
+    halo_start(LOADS_W, east, r0[0])
+    halo_start(LOADS_N, south, r0[1])
+
     fetches[1].wait()
 
     def permute(step, _):
@@ -334,39 +357,31 @@
         for d in range(4):
             at = ((y_at * LZ + half * 4 + d) * 2 + j_half) * FP
             tiles.append(coarse_v[:, pl.ds(pl.multiple_of(at, FP), FP)])
-        for q in range(4):
-            mixed = tiles[q] if q == 0 else pltpu.roll(tiles[0], ((0 - q) % 4) * 32, 1)
-            for d in range(1, 4):
-                turn = ((d - q) % 4) * 32
-                turned = pltpu.roll(tiles[d], turn, 1) if turn else tiles[d]
-                mixed = jnp.where(lane_group == d, turned, mixed)
+        for q, mixed in enumerate(transpose_groups(tiles, lane_group)):
             at = (y_at * LX + j_half * 2 + q // 2) * 256 + half * FP
             permuted[q % 2, :, pl.ds(pl.multiple_of(at, FP), FP)] = mixed
         return 0
 
     lax.fori_loop(0, 16, permute, 0)
-    fetches[2].wait()
-    c_high[...], c_low[...] = split(coupling_v[...])
-
-    pl.semaphore_wait(barrier, len(greeted) - 1 + LZ * lax.div(LZ - 1 - z, LZ - 1))
-
-    gather_start(0, r0, None, None)
-    halo_start(LOADS_W, east, r0[0])
-    halo_start(LOADS_N, south, r0[1])
     swap = pltpu.make_async_remote_copy(
         permuted.at[1 - core], partner_rows, swap_send, swap_recv, device_id=partner, device_id_type=MESH
     )
     go(swap)
 
+    def interior_columns(columns):
+        i_high, i_low = split(interior_v[:, columns])
+        both = dot(c_parts[...], i_high)
+        total = both[:NF] + both[NF:] + dot(c_parts[:NF], i_low)
+        t_parts[:NF, columns], t_parts[NF:, columns] = split(total)
+
     def times_interior(step, _):
-        columns = pl.ds(pl.multiple_of(step * COLS, FP), COLS)
-        i_high[...], i_low[...] = split(interior_v[:, columns])
-        total = dot(c_high[...], i_high[...]) + dot(c_low[...], i_high[...]) + dot(c_high[...], i_low[...])
-        t_high[:, columns], t_low[:, columns] = split(total)
+        interior_columns(pl.ds(pl.multiple_of(step * COLS, FP), COLS))
         return 0
 
+    fetches[2].wait()
+    c_parts[:NF], c_parts[NF:] = split(coupling_v[...])
     fetches[3].wait()
-    lax.fori_loop(0, 1, times_interior, 0)
+    lax.fori_loop(0, 2, times_interior, 0)
 
     fetches[4].wait()
     pad_split(lambda a, b: local_v[a * F : (a + 1) * F, b * F : (b + 1) * F], l_high, l_low)
@@ -386,8 +401,10 @@
     place_rows(permuted[core], core * 32)
     swap.wait_recv()
     place_rows(partner_rows[...], (1 - core) * 32)
-    lax.fori_loop(1, NI // COLS, times_interior, 0)
-    back = dot_t(t_high[...], c_high[...]) + dot_t(t_low[...], c_high[...]) + dot_t(t_high[...], c_low[...])
+    lax.fori_loop(2, NI // COLS, times_interior, 0)
+    interior_columns(slice(NI // COLS * COLS, NI))
+    back = dot_t(t_parts[...], c_parts[:NF])
+    back = back[:NF] + back[NF:] + dot_t(t_parts[:NF], c_parts[NF:])
     fetches[5].wait()
     schur_v[...] = bound_v[...] - back
     pad_split(lambda a, b: schur_v[a * F : (a + 1) * F, b * F : (b + 1) * F], s_high, s_low)
@@ -404,9 +421,12 @@
     spread_faces(PRE1, w0_local)
     gather_forward(1, True)
     w0_local = total_faces(PRE1, w0_local)
-    wide, column = gather_finish(1, False)
-    rz0, dq0 = column(0), column(1)
-    step0 = rz0 / dq0
+
+    def first_step(column):
+        rz0, dq0 = column(0), column(1)
+        return rz0, dq0, rz0 / dq0
+
+    wide, (rz0, dq0, step0) = gather_finish(1, False, first_step)
     w0 = [a + b for a, b in zip(w0_local, wide)]
     z1 = inner_faces([a - step0 * b for a, b in zip(z0, w0)])
 
@@ -420,13 +440,16 @@
     spread_faces(PRE2, w1_local, True)
     gather_forward(2, True)
     w1_local = total_faces(PRE2, w1_local, True)
-    wide, column = gather_finish(2, True)
+
+    def second_step(column):
+        rz1 = column(0)
+        ratio = rz1 / rz0
+        return ratio, rz1 / (column(1) + ratio * (column(2) + column(3)) + ratio * ratio * dq0)
+
+    wide, (ratio, step1) = gather_finish(2, True, second_step)
     w1 = [a + b for a, b in zip(w1_local, wide)]
 
     t1, w0 = owned(t1_faces), owned(w0)
-    rz1 = column(0)
-    ratio = rz1 / rz0
-    step1 = rz1 / (column(1) + ratio * (column(2) + column(3)) + ratio * ratio * dq0)
     for f in range(2):
         place = slice(f * FP, (f + 1) * FP)
         direction = z1_own[f] + ratio * z0_own[f]
@@ -469,12 +492,8 @@
             pltpu.VMEM((NP, NP), bf16),
             pltpu.VMEM((NP, NP), bf16),
             pltpu.VMEM((NP, NP), bf16),
-            pltpu.VMEM((NF, NI), bf16),
-            pltpu.VMEM((NF, NI), bf16),
-            pltpu.VMEM((NI, COLS), bf16),
-            pltpu.VMEM((NI, COLS), bf16),
-            pltpu.VMEM((NF, NI), bf16),
-            pltpu.VMEM((NF, NI), bf16),
+            pltpu.VMEM((2 * NF, NI), bf16),
+            pltpu.VMEM((2 * NF, NI), bf16),
             pltpu.VMEM((NF, NF), f32),
             pltpu.VMEM((2, 32, NC // 2), f32),
             pltpu.VMEM((32, NC // 2), f32),
@@ -486,8 +505,8 @@
             pltpu.VMEM((3, LZ, 4, FP), f32),
             pltpu.VMEM((3, 8, FP), f32),
             pltpu.VMEM((3, LX * LY, 40, FP), f32),
-            pltpu.VMEM((3, 24, FP), f32),
-            pltpu.VMEM((3, 5, 24, FP), f32),
+            pltpu.VMEM((3, 16, FP), f32),
+            pltpu.VMEM((3, 5, 16, FP), f32),
             pltpu.VMEM((SLOTS, K, FP), f32),
             pltpu.VMEM((SLOTS, K, FP), f32),
             dma((3, LZ)),

time: 63.6 us -> 62.7 us (0.986)
  Pallas kernels: 62.8 us -> 61.9 us
    pallas_call x1, Pallas kernels: 61.3 us -> 60.4 us  [shards(): pl.pallas_call(kernel, out_shape=jax.ShapeDtypeStruct((3, K, 2 * FP), f32...]
where the time goes in v3:
time: 62.7 us; the launch traced here: 62.5 us
  Pallas kernels  61.9 us (99%)
  between operations  0.64 us (1%)
    pallas_call x1, Pallas kernels, shards(): pl.pallas_call(kernel, out_shape=jax.ShapeDtypeStruct((3, K, 2 * FP), f32...  60.4 us
    pallas_call x1, Pallas kernels, shards(): return pl.pallas_call(unpad, out_shape=(out, out, out))(packed)  1.49 us

profile of v3, /device:TPU:1, one launch (start us, length us, event | category | flops | bytes accessed | tf_op | source)
XLA Modules:
  0.0 62.5 jit_solution(3591126736175008254)
XLA Ops:
  0.6 60.4 %shard_map.85.packed_ref = f32[3,16,256]{2,1,0:T(8,128)} custom-call(f32[1,1,16,192]{3,2,1,0:T(8,128)} %loads_ref.1, f32[1,1,384,384]{3,2,1,0:T(8,128)} %bound_ref.1, f32[1,1,384,1152]{3,2,1,0:T(8,128)} %coupling_ref.1, f32[1,1,1152,1152]{3,2,1,0:T(8,128)} %interior_ref.1, f32[1,1,384,384]{3,2,1,0:T(8,128)} %local_ref.1, f32[32,8192]{1,0:T(8,128)} %coarse_ref.1), custom_call_target="tpu_custom_call" | custom-call | tf_op jit(solution)/shard_map/pallas_call | solution.py:478
  61.1 1.5 %shard_map.86 = (f32[1,1,16,192]{3,2,1,0:T(8,128)}, f32[1,1,16,192]{3,2,1,0:T(8,128)}, f32[1,1,16,192]{3,2,1,0:T(8,128)}) custom-call(f32[3,16,256]{2,1,0:T(8,128)} %shard_map.85.packed_ref), custom_call_target="tpu_custom_call" | custom-call | tf_op jit(solution)/shard_map/pallas_call | solution.py:532

commit v4 on v3

--- a/solution.py
+++ b/solution.py
@@ -269,7 +269,7 @@
     def gather_finish(phase, last, scalars=None):
         total = jnp.zeros((2 * K, FP), f32)
         sums = jnp.zeros((8, FP), f32)
-        for group in (PLANE_ORDER[:11], PLANE_ORDER[11:]):
+        for group in (PLANE_ORDER[:5], PLANE_ORDER[5:11], PLANE_ORDER[11:]):
             for s in group:
                 if s:
                     plane_copy(phase, s).wait_recv()
@@ -342,12 +342,6 @@
         jnp.concatenate([loads_v[:, F : 2 * F], padding], axis=1),
     ]
 
-    pl.semaphore_wait(barrier, len(greeted) - 1 + LZ * lax.div(LZ - 1 - z, LZ - 1))
-
-    gather_start(0, r0, None, None)
-    halo_start(LOADS_W, east, r0[0])
-    halo_start(LOADS_N, south, r0[1])
-
     fetches[1].wait()
 
     def permute(step, _):
@@ -363,6 +357,12 @@
         return 0
 
     lax.fori_loop(0, 16, permute, 0)
+    pl.semaphore_wait(barrier, len(greeted) - 1 + LZ * lax.div(LZ - 1 - z, LZ - 1))
+
+    gather_start(0, r0, None, None)
+    halo_start(LOADS_W, east, r0[0])
+    halo_start(LOADS_N, south, r0[1])
+
     swap = pltpu.make_async_remote_copy(
         permuted.at[1 - core], partner_rows, swap_send, swap_recv, device_id=partner, device_id_type=MESH
     )

time: 62.7 us -> 61.8 us (0.986)
  Pallas kernels: 61.9 us -> 61 us
    pallas_call x1, Pallas kernels: 60.4 us -> 59.5 us  [shards(): pl.pallas_call(kernel, out_shape=jax.ShapeDtypeStruct((3, K, 2 * FP), f32...]
where the time goes in v4:
time: 61.8 us; the launch traced here: 61.6 us
  Pallas kernels  61 us (99%)
  between operations  0.64 us (1%)
    pallas_call x1, Pallas kernels, shards(): pl.pallas_call(kernel, out_shape=jax.ShapeDtypeStruct((3, K, 2 * FP), f32...  59.5 us
    pallas_call x1, Pallas kernels, shards(): return pl.pallas_call(unpad, out_shape=(out, out, out))(packed)  1.49 us

profile of v4, /device:TPU:1, one launch (start us, length us, event | category | flops | bytes accessed | tf_op | source)
XLA Modules:
  0.0 61.6 jit_solution(13363296701497920054)
XLA Ops:
  0.6 59.5 %shard_map.85.packed_ref = f32[3,16,256]{2,1,0:T(8,128)} custom-call(f32[1,1,16,192]{3,2,1,0:T(8,128)} %loads_ref.1, f32[1,1,384,384]{3,2,1,0:T(8,128)} %bound_ref.1, f32[1,1,384,1152]{3,2,1,0:T(8,128)} %coupling_ref.1, f32[1,1,1152,1152]{3,2,1,0:T(8,128)} %interior_ref.1, f32[1,1,384,384]{3,2,1,0:T(8,128)} %local_ref.1, f32[32,8192]{1,0:T(8,128)} %coarse_ref.1), custom_call_target="tpu_custom_call" | custom-call | tf_op jit(solution)/shard_map/pallas_call | solution.py:478
  60.1 1.5 %shard_map.86 = (f32[1,1,16,192]{3,2,1,0:T(8,128)}, f32[1,1,16,192]{3,2,1,0:T(8,128)}, f32[1,1,16,192]{3,2,1,0:T(8,128)}) custom-call(f32[3,16,256]{2,1,0:T(8,128)} %shard_map.85.packed_ref), custom_call_target="tpu_custom_call" | custom-call | tf_op jit(solution)/shard_map/pallas_call | solution.py:532

commit v5 on v4

--- a/solution.py
+++ b/solution.py
@@ -205,6 +205,10 @@
             packed = jnp.where(lane_group == q, sums[4 * q : 4 * q + 4], packed)
         return packed
 
+    def line_start(phase):
+        for s in LINE_ORDER[:0:-1]:
+            go(line_copy(phase, s))
+
     def gather_start(phase, own, shared, dots):
         values = [jnp.concatenate(own, axis=1)] + ([jnp.concatenate(shared, axis=1)] if shared else [])
         high, low = split(jnp.concatenate(values, axis=0))
@@ -233,8 +237,8 @@
                 for s in range(LZ):
                     head_copy(phase, s).start()
 
-        for s in LINE_ORDER[:0:-1]:
-            go(line_copy(phase, s))
+        if shared:
+            line_start(phase)
 
     def gather_forward(phase, shared):
         for s in range(1, LZ):
@@ -342,6 +346,8 @@
         jnp.concatenate([loads_v[:, F : 2 * F], padding], axis=1),
     ]
 
+    gather_start(0, r0, None, None)
+
     fetches[1].wait()
 
     def permute(step, _):
@@ -359,7 +365,7 @@
     lax.fori_loop(0, 16, permute, 0)
     pl.semaphore_wait(barrier, len(greeted) - 1 + LZ * lax.div(LZ - 1 - z, LZ - 1))
 
-    gather_start(0, r0, None, None)
+    line_start(0)
     halo_start(LOADS_W, east, r0[0])
     halo_start(LOADS_N, south, r0[1])
 

time: 61.8 us -> 61.8 us (level)
  no operation moved by 1% of the time
where the time goes in v5:
time: 61.8 us; the launch traced here: 61.6 us
  Pallas kernels  61 us (99%)
  between operations  0.64 us (1%)
    pallas_call x1, Pallas kernels, shards(): pl.pallas_call(kernel, out_shape=jax.ShapeDtypeStruct((3, K, 2 * FP), f32...  59.5 us
    pallas_call x1, Pallas kernels, shards(): return pl.pallas_call(unpad, out_shape=(out, out, out))(packed)  1.49 us

profile of v5, /device:TPU:1, one launch (start us, length us, event | category | flops | bytes accessed | tf_op | source)
XLA Modules:
  0.0 61.6 jit_solution(6210821721830775895)
XLA Ops:
  0.6 59.5 %shard_map.85.packed_ref = f32[3,16,256]{2,1,0:T(8,128)} custom-call(f32[1,1,16,192]{3,2,1,0:T(8,128)} %loads_ref.1, f32[1,1,384,384]{3,2,1,0:T(8,128)} %bound_ref.1, f32[1,1,384,1152]{3,2,1,0:T(8,128)} %coupling_ref.1, f32[1,1,1152,1152]{3,2,1,0:T(8,128)} %interior_ref.1, f32[1,1,384,384]{3,2,1,0:T(8,128)} %local_ref.1, f32[32,8192]{1,0:T(8,128)} %coarse_ref.1), custom_call_target="tpu_custom_call" | custom-call | tf_op jit(solution)/shard_map/pallas_call | solution.py:484
  60.1 1.5 %shard_map.86 = (f32[1,1,16,192]{3,2,1,0:T(8,128)}, f32[1,1,16,192]{3,2,1,0:T(8,128)}, f32[1,1,16,192]{3,2,1,0:T(8,128)}) custom-call(f32[3,16,256]{2,1,0:T(8,128)} %shard_map.85.packed_ref), custom_call_target="tpu_custom_call" | custom-call | tf_op jit(solution)/shard_map/pallas_call | solution.py:538
